TPU v7x, 512 devices: a whole 4x4x16 slice. The times are simulated.
512 devices in a mesh: dom: 16 (over z_lo, core), rep: 32 (over x, z_hi, y).
Axes of the slice: x: 4, y: 4, z: 16 (z_hi: 2, z_lo: 8; z = z_hi * 8 + z_lo), core: 2. Of those that a mesh axis runs over, the one named last changes fastest.
Arguments:
- cells: int32 [3, 8388608], P(None, ('dom', 'rep')), may hold values from 0 to 191, as said below
- offsets: float32 [3, 8388608], P(None, ('dom', 'rep')), may hold values from 0 to 1
- displacements: float32 [3, 8388608], P(None, ('dom', 'rep')), may hold values from -1 to 1
- block_split: int32 [262144], P(('dom', 'rep')), may hold values from 8 to 24
- fields: float32 [2, 32, 36864], P(None, 'dom'), may hold values from -12 to 12
- crossing: int32 [512, 2, 16], P(('dom', 'rep')), may hold values from 0 to 511, as said below
- crossing_counts: int32 [512, 2], P(('dom', 'rep')), may hold values from 0 to 16, as said below
Outputs:
- new_offsets: float32 [3, 8388608], P(None, ('dom', 'rep'))
- density: float32 [2, 32, 36864], P(None, 'dom', 'rep')
- arrivals: float32 [2, 3, 262144], P(None, None, ('dom', 'rep'))
Inputs may be any that keep to these rules, and one draw needn't show every extreme that they name: x and y cells 0 to 191, z the layer 0 to 1 within the bead's domain; consecutive beads of a chain lie at most one cell apart along each direction (x and y periodically). `crossing`: the 32 entries of one device are distinct chain indices of that device. `crossing_counts`: the used slots are the first ones.
All inputs are finite; a program needn't handle non-finite values.
Results may differ from a plain program's by a relative error of at most 0.0003.
Values sent between devices are 32-bit elements; how exact they have to be, the bound alone decides.
No kernel may reach another device: no remote copies, remote signals or barrier semaphores. Data moves between devices by JAX's collectives and lax.ppermute only.
A program may use at most 192 MiB of HBM per device.

v0:
```python
import jax
import jax.numpy as jnp
from jax import lax
from jax.sharding import PartitionSpec as P

GRID = 192


MOBILITY = 0.1


def shifted_2(value, axis, steps):
    count = lax.axis_size(axis)
    pairs = [(source, (source + steps) % count) for source in range(count)]
    return lax.ppermute(value, axis, pairs)


def padded_2(cells, sides, width):
    for axis, dim in sides:
        count = lax.axis_size(axis)
        head = lax.slice_in_dim(cells, 0, width, axis=dim)
        tail = lax.slice_in_dim(cells, cells.shape[dim] - width, cells.shape[dim], axis=dim)
        cells = jnp.concatenate(
            [
                lax.ppermute(tail, axis, [(i, (i + 1) % count) for i in range(count)]),
                cells,
                lax.ppermute(head, axis, [((i + 1) % count, i) for i in range(count)]),
            ],
            axis=dim,
        )
    return cells


def wrap_gap(stride_gap, period):
    return (stride_gap + period // 2) % period - period // 2


def bond_force(cell_rows, offset_rows):
    stride_gap = cell_rows[:, 1:] - cell_rows[:, :-1]
    plane_gap = wrap_gap(stride_gap[:2], GRID)
    stride_gap = jnp.concatenate([plane_gap, stride_gap[2:]], axis=0).astype(jnp.float32)
    stride_gap = stride_gap + (offset_rows[:, 1:] - offset_rows[:, :-1])
    zeros_row = jnp.zeros_like(stride_gap[:, :1])
    return jnp.concatenate([stride_gap, zeros_row], axis=1) - jnp.concatenate(
        [zeros_row, stride_gap], axis=1
    )


def field_forces(padded):
    interior = padded[:, 1:-1]
    layer_count = interior.shape[1]
    force_z = (padded[:, :-2] - padded[:, 2:]) * 0.5
    square = interior.reshape(2, layer_count, GRID, GRID)
    force_x = ((jnp.roll(square, 1, 2) - jnp.roll(square, -1, 2)) * 0.5).reshape(
        2, layer_count, GRID * GRID
    )
    force_y = ((jnp.roll(square, 1, 3) - jnp.roll(square, -1, 3)) * 0.5).reshape(
        2, layer_count, GRID * GRID
    )
    return jnp.stack([force_x, force_y, force_z]).reshape(3, -1)


def move_beads(cell_rows, offset_rows, displace_rows, split_rows, forces, layer_count):
    bead_count = cell_rows.shape[1]
    positions_along = jnp.arange(bead_count, dtype=jnp.int32)[:, None]
    species = (positions_along >= split_rows[None, :]).astype(jnp.int32)
    plane_index = cell_rows[0] * GRID + cell_rows[1]
    layer_of = cell_rows[2]
    lookup = species * (layer_count * GRID * GRID) + layer_of * (GRID * GRID) + plane_index
    field_push = forces[:, lookup]
    shifted = (
        offset_rows + MOBILITY * (bond_force(cell_rows, offset_rows) + field_push) + displace_rows
    )
    return (shifted, species, plane_index, layer_of)


def deposit(shifted, species, plane_index, layer_of, layer_count):
    upper_share = jnp.clip(shifted[2], 0.0, 1.0)
    base_index = species * (layer_count * GRID * GRID) + plane_index
    lower_index = (base_index + layer_of * (GRID * GRID)).reshape(-1)
    upper_index = (base_index + (layer_of + 1) * (GRID * GRID)).reshape(-1)
    all_index = jnp.concatenate([lower_index, upper_index])
    all_weight = jnp.concatenate([(1.0 - upper_share).reshape(-1), upper_share.reshape(-1)])
    grid_sum = jnp.zeros((2 * layer_count * GRID * GRID,), jnp.float32)
    return grid_sum.at[all_index].add(all_weight)


def crossing_rows(cell_rows, shifted, chosen, count_used, lift_by):
    position = cell_rows.astype(jnp.float32) + shifted
    picked = jnp.take(position, chosen, axis=2)
    picked = picked.at[2].add(lift_by)
    kept_mask = (jnp.arange(chosen.shape[0], dtype=jnp.int32) < count_used).astype(jnp.float32)
    return (picked * kept_mask).reshape(3, -1)


def send_up(rim_layer, rising):
    return shifted_2((rim_layer, rising), "dom", 1)


def reduce_grid(grid_sum):
    summed_all = lax.psum(grid_sum, "rep")
    share_width = grid_sum.shape[2] // lax.axis_size("rep")
    return lax.dynamic_slice_in_dim(summed_all, lax.axis_index("rep") * share_width, share_width, 2)


def shards(cells, offsets, displacements, block_split, fields, crossing, crossing_counts):
    chain_count = block_split.shape[0]
    bead_count = cells.shape[1] // chain_count
    layer_count = fields.shape[1]
    plane_size = GRID * GRID
    cell_rows = cells.reshape(3, bead_count, chain_count)
    offset_rows = offsets.reshape(3, bead_count, chain_count)
    displace_rows = displacements.reshape(3, bead_count, chain_count)
    padded = padded_2(fields, (("dom", 1),), 1)
    forces = field_forces(padded)
    shifted, species, plane_index, layer_of = move_beads(
        cell_rows, offset_rows, displace_rows, block_split, forces, layer_count
    )
    partial_grid = deposit(shifted, species, plane_index, layer_of, layer_count + 1).reshape(
        2, layer_count + 1, plane_size
    )
    rising = crossing_rows(
        cell_rows, shifted, crossing[0, 0], crossing_counts[0, 0], -float(layer_count)
    )
    falling = crossing_rows(
        cell_rows, shifted, crossing[0, 1], crossing_counts[0, 1], float(layer_count)
    )
    carried, arrived_up = send_up(partial_grid[:, layer_count:], rising)
    grid_sum = jnp.concatenate(
        [partial_grid[:, :1] + carried, partial_grid[:, 1:layer_count]], axis=1
    )
    density_sum = reduce_grid(grid_sum)
    arrived_down = shifted_2(falling, "dom", -1)
    density_scale = GRID * GRID * layer_count / (lax.axis_size("rep") * chain_count * bead_count)
    return (
        shifted.reshape(3, -1),
        density_sum * density_scale,
        jnp.stack([arrived_up, arrived_down]),
    )


def solution(mesh):
    in_specs = (
        P(None, ("dom", "rep")),
        P(None, ("dom", "rep")),
        P(None, ("dom", "rep")),
        P(("dom", "rep")),
        P(None, "dom", None),
        P(("dom", "rep"), None, None),
        P(("dom", "rep"), None),
    )
    out_specs = (P(None, ("dom", "rep")), P(None, "dom", "rep"), P(None, None, ("dom", "rep")))
    return jax.shard_map(shards, mesh=mesh, in_specs=in_specs, out_specs=out_specs, check_vma=False)
```

profile of v0, /device:TPU:1, one launch (start us, length us, event | category | flops | bytes accessed | tf_op | source)
XLA Modules:
  0.0 1071.7 jit_solution(11430047238189971474)
XLA Ops:
  7.2 1.8 fusion.22
  9.1 0.9 copy.75
  10.0 4.9 collective-permute-start
  14.9 0.9 copy.76
  15.9 5.8 collective-permute-start.1
  21.6 0.6 reshape.439
  22.2 0.3 fusion.20
  22.5 0.2 fusion.21
  22.8 0.6 copy-done.1
  23.4 1.6 slice_multiply_fusion
  25.1 0.7 fusion.9
  25.8 0.4 fusion.1
  26.2 0.7 mul.172
  27.2 1.6 mul.170
  28.8 0.9 mul.178
  29.6 0.9 fusion.11
  30.5 0.6 broadcast_clamp_fusion
  31.2 1.0 copy.101
  32.3 0.6 fusion.23
  32.8 1.1 compare_convert_fusion.1
  34.0 0.8 compare_select_fusion
  34.8 1.2 compare_convert_fusion
  36.0 0.7 fusion.6
  36.7 1.3 copy.62
  38.0 1.3 copy.64
  39.3 1.1 fusion.3
  40.4 0.9 stack.15
  41.3 2.6 pad_maximum_fusion
  43.9 34.2 %copy.65 = f32[3,147456]{0,1:T(8,128)} copy(f32[3,147456]{1,0:T(4,128)S(1)} %pad_maximum_fusion) | data formatting | bytes 3538944 | tf_op jit(solution)/shard_map/stack | solution.py:60
  78.1 237.5 %gather_fusion = f32[16384,3]{1,0:T(8,128)} fusion(f32[3,147456]{0,1:T(8,128)} %copy.65, s32[16384]{0:T(1024)S(1)} %copy-done.8), kind=kCustom, calls=%fused_computation.2 | custom fusion | bytes 458752 | tf_op jit(solution)/shard_map/gather | solution.py:70
  315.6 5.3 copy.74
  321.0 0.2 convert_add_fusion
  321.2 0.4 copy.67
  321.6 0.6 gather_fusion.1
  322.2 0.6 gather_fusion.2
  322.8 171.5 %scatter_custom_fusion = f32[221184]{0:T(1024)S(1)} fusion(s32[32768]{0:T(1024)} %bitcast.86, f32[32768]{0:T(1024)S(1)} %pad_maximum_fusion.4, f32[]{:T(128)} %constant.101.clone.1), kind=kCustom, calls=%fused_computation.15 | custom fusion | flops 32768 | bytes 885248 | tf_op jit(solution)/shard_map/scatter-add | solution.py:85
  494.3 0.4 reshape.442
  494.8 0.3 slice.197
  495.1 1.9 collective-permute-start.2
  497.1 9.4 collective-permute-done.2
  506.5 0.5 slice_add_fusion
  507.0 1.4 pad_maximum_fusion.3
  508.6 1.9 collective-permute-start.3
  510.8 13.7 %collective-permute-start.4 = (f32[3,512]{1,0:T(4,128)S(1)}, f32[3,512]{1,0:T(4,128)S(1)}, u32[]{:S(2)}, u32[]{:S(2)}) collective-permute-start(f32[3,512]{1,0:T(4,128)S(1)} %reshape.444), channel_id=1, source_target_pairs={{0,480},{32,0},{64,32},{96,64},{128,96},{160,128},{192,160},{224,1... | collective-permute-start | bytes 18440 | tf_op jit(solution)/shard_map/ppermute | solution.py:15
  524.5 0.8 copy.81
  525.4 0.6 copy.73
  526.0 537.5 %all-reduce.4.cloned.1.call-done = f32[2,2,36864]{2,1,0:T(2,128)} async-done(((f32[2,2,36864]{2,1,0:T(2,128)}), f32[2,2,36864]{2,1,0:T(2,128)}) %all-reduce.4.cloned.1.call-update) | async-done | bytes 589840 | tf_op jit(solution)/shard_map/psum | solution.py:101
  1063.5 1.3 dynamic-slice_multiply_fusion
  (67 shorter events, 1.2 us)
Async XLA Ops:
  7.2 14.5 %copy-start = (f32[2,2,36864]{2,1,0:T(2,128)S(1)}, f32[2,2,36864]{2,1,0:T(2,128)}, u32[]{:S(2)}) copy-start(f32[2,2,36864]{2,1,0:T(2,128)} %param.17) | copy-start | bytes 1769476
  7.2 1056.3 %all-reduce.4.cloned.1.call-start = ((), (), s32[]{:S(2)}) async-start(), calls=%async_computation | async-start | bytes 1179648 | tf_op jit(solution)/shard_map/psum | solution.py:101
  10.0 26.7 %collective-permute-start = (f32[2,1,36864]{2,0,1:T(2,128)}, f32[2,1,36864]{2,0,1:T(2,128)}, u32[]{:S(2)}, u32[]{:S(2)}) collective-permute-start(f32[2,1,36864]{2,0,1:T(2,128)} %copy.75), channel_id=1, source_target_pairs={{0,32},{32,64},{64,96},{96,128},{128,160},{160,192},{192,224},{224... | collective-permute-start | bytes 884744 | tf_op jit(solution)/shard_map/ppermute | solution.py:25
  15.9 22.1 %collective-permute-start.1 = (f32[2,1,36864]{2,0,1:T(2,128)}, f32[2,1,36864]{2,0,1:T(2,128)}, u32[]{:S(2)}, u32[]{:S(2)}) collective-permute-start(f32[2,1,36864]{2,0,1:T(2,128)} %copy.76), channel_id=1, source_target_pairs={{32,0},{64,32},{96,64},{128,96},{160,128},{192,160},{224,192},{256... | collective-permute-start | bytes 884744 | tf_op jit(solution)/shard_map/ppermute | solution.py:27
  22.5 1.0 copy-start.1
  25.1 0.7 copy-start.5
  26.2 3.4 copy-start.12
  27.1 5.1 copy-start.14
  27.1 5.1 copy-start.13
  27.1 6.9 copy-start.6
  27.1 6.9 copy-start.9
  27.2 6.9 copy-start.10
  27.2 8.8 slice-start
  27.2 8.8 copy-start.7
  43.9 34.2 %copy-start.8 = (s32[16384]{0:T(1024)S(1)}, s32[16384]{0:T(1024)}, u32[]{:S(2)}) copy-start(s32[16384]{0:T(1024)} %broadcast_clamp_fusion) | copy-start | bytes 196612
  315.6 5.3 copy-start.2
  315.6 5.3 copy-start.3
  315.6 5.4 copy-start.4
  315.6 5.4 copy-start.11
  494.7 13.6 %copy-start.15 = (f32[16]{0:T(128)S(1)}, f32[16]{0:T(128)}, u32[]{:S(2)}) copy-start(f32[16]{0:T(128)} %compare_convert_fusion.1) | copy-start | bytes 196
  494.7 15.8 %copy-start.16 = (f32[16]{0:T(128)S(1)}, f32[16]{0:T(128)}, u32[]{:S(2)}) copy-start(f32[16]{0:T(128)} %compare_convert_fusion) | copy-start | bytes 196
  495.1 11.4 %collective-permute-start.2 = (f32[2,1,36864]{2,1,0:T(1,128)S(1)}, f32[2,1,36864]{2,1,0:T(1,128)S(1)}, u32[]{:S(2)}, u32[]{:S(2)}) collective-permute-start(f32[2,1,36864]{2,1,0:T(1,128)S(1)} %slice.197), channel_id=1, source_target_pairs={{0,32},{32,64},{64,96},{96,128},{128,160},{160,192},{192,224},{224... | collective-permute-start | bytes 884744 | tf_op jit(solution)/shard_map/ppermute | solution.py:15
  508.6 16.7 %collective-permute-start.3 = (f32[3,512]{1,0:T(4,128)S(1)}, f32[3,512]{1,0:T(4,128)S(1)}, u32[]{:S(2)}, u32[]{:S(2)}) collective-permute-start(f32[3,512]{1,0:T(4,128)S(1)} %reshape.443), channel_id=1, source_target_pairs={{0,32},{32,64},{64,96},{96,128},{128,160},{160,192},{192,224},{224... | collective-permute-start | bytes 18440 | tf_op jit(solution)/shard_map/ppermute | solution.py:15
  510.8 14.5 %collective-permute-start.4 = (f32[3,512]{1,0:T(4,128)S(1)}, f32[3,512]{1,0:T(4,128)S(1)}, u32[]{:S(2)}, u32[]{:S(2)}) collective-permute-start(f32[3,512]{1,0:T(4,128)S(1)} %reshape.444), channel_id=1, source_target_pairs={{0,480},{32,0},{64,32},{96,64},{128,96},{160,128},{192,160},{224,1... | collective-permute-start | bytes 18440 | tf_op jit(solution)/shard_map/ppermute | solution.py:15
Sparse Core Ops, SparseCore 0:
  508.5 554.9 all-reduce.3
where the time goes:
time: 1090 us; the launch traced here: 1070 us
  waiting for transfers between devices  547 us (50%)
  local copies, waits for them, and re-layouts  295 us (27%)
  other arithmetic  187 us (17%)
  starting transfers between devices  28.2 us (3%)
  between operations  14.6 us (1%)
    psum x1, waiting for transfers between devices, reduce_grid(): summed_all = lax.psum(grid_sum, 'rep')  537 us
    gather x2, local copies, waits for them, and re-layouts, move_beads(): field_push = forces[:, lookup]  243 us
    scatter-add x1, other arithmetic, deposit(): return grid_sum.at[all_index].add(all_weight)  171 us
    another operation x2, local copies, waits for them, and re-layouts, field_forces(): return jnp.stack([force_x, force_y, force_z]).reshape(3, -1)  35.1 us
  transfers between devices with their start and end apart: 6, of which 2 were waited for; matrix products, arithmetic and copies ran while one was open for 2% of the time, Pallas kernels for 0%

commit v1 on v0

v1 whole, which is shorter than its diff:
```python
import functools

import jax
import jax.numpy as jnp
from jax import lax
from jax.experimental import pallas as pl
from jax.experimental.pallas import tpu as pltpu
from jax.sharding import PartitionSpec as P

GRID = 192
MOBILITY = 0.1
HEAD_BEADS = 8
TAIL_BEAD = 24


def split_two(value):
    high = value.astype(jnp.bfloat16)
    low = (value - high.astype(jnp.float32)).astype(jnp.bfloat16)
    return high, low


def split_three(value):
    high, rest = value.astype(jnp.bfloat16), None
    rest = value - high.astype(jnp.float32)
    mid = rest.astype(jnp.bfloat16)
    low = (rest - mid.astype(jnp.float32)).astype(jnp.bfloat16)
    return high, mid, low


def wrap_gap(gap):
    gap = jnp.where(gap >= GRID // 2, gap - GRID, gap)
    return jnp.where(gap < -(GRID // 2), gap + GRID, gap)


def table_rows(field_ref, below_ref, above_ref, layers):
    parts = [[], [], []]
    for species in range(2):
        planes = [field_ref[species, layer] for layer in range(layers)]
        stack = [below_ref[species]] + planes + [above_ref[species]]
        for layer in range(layers):
            plane = planes[layer]
            back_x = jnp.concatenate([plane[-1:], plane[:-1]], axis=0)
            fore_x = jnp.concatenate([plane[1:], plane[:1]], axis=0)
            back_y = jnp.concatenate([plane[:, -1:], plane[:, :-1]], axis=1)
            fore_y = jnp.concatenate([plane[:, 1:], plane[:, :1]], axis=1)
            parts[0].append((back_x - fore_x) * 0.5)
            parts[1].append((back_y - fore_y) * 0.5)
            parts[2].append((stack[layer] - stack[layer + 2]) * 0.5)
    return [jnp.concatenate(part, axis=1) for part in parts]


def step_kernel(
    layers, beads, chains, cells_ref, offsets_ref, displace_ref, split_ref, field_ref, below_ref,
    above_ref, chosen_ref, used_ref, new_ref, sums_ref, carry_ref, picked_ref,
    table_ref, hot_ref, weight_ref, total_ref, place_ref,
):
    group = hot_ref.shape[1] // chains
    width = 2 * layers * GRID
    half = layers * GRID
    for k, table in enumerate(table_rows(field_ref, below_ref, above_ref, layers)):
        high, low = split_two(table)
        table_ref[k * GRID:(k + 1) * GRID, :] = high
        table_ref[(3 + k) * GRID:(4 + k) * GRID, :] = low
    total_ref[...] = jnp.zeros_like(total_ref)

    def one_bead(j, slot, first, size):
        def row(ref, k, bead):
            return ref[k:k + 1, pl.ds(pl.multiple_of(bead * chains, chains), chains)]

        before = jnp.maximum(j - 1, 0)
        after = jnp.minimum(j + 1, beads - 1)
        x, y, z = (row(cells_ref, k, j) for k in range(3))
        key = z * GRID + y
        if size == width:
            key = key + jnp.where(j >= split_ref[...], half, 0)
        hot = lax.broadcasted_iota(jnp.int32, (size, chains), 0) == key
        hot = jnp.where(hot, 1.0, 0.0).astype(jnp.bfloat16)
        lanes = slice(slot * chains, (slot + 1) * chains)
        hot_ref[0:size, lanes] = hot
        rows = jnp.dot(table_ref[:, first:first + size], hot, preferred_element_type=jnp.float32)
        mask = lax.broadcasted_iota(jnp.int32, (GRID, chains), 0) == x
        moved = []
        for k in range(3):
            pair = rows[k * GRID:(k + 1) * GRID] + rows[(3 + k) * GRID:(4 + k) * GRID]
            push = jnp.sum(jnp.where(mask, pair, 0.0), axis=0, keepdims=True)
            cell, off = row(cells_ref, k, j), row(offsets_ref, k, j)
            gap_after = row(cells_ref, k, after) - cell
            gap_before = cell - row(cells_ref, k, before)
            if k < 2:
                gap_after, gap_before = wrap_gap(gap_after), wrap_gap(gap_before)
            gap_after = gap_after.astype(jnp.float32) + (row(offsets_ref, k, after) - off)
            gap_before = gap_before.astype(jnp.float32) + (off - row(offsets_ref, k, before))
            bond = gap_after - gap_before
            new = off + MOBILITY * (bond + push) + row(displace_ref, k, j)
            new_ref[k:k + 1, pl.ds(pl.multiple_of(j * chains, chains), chains)] = new
            place_ref[k, pl.ds(j, 1), :] = cell.astype(jnp.float32) + new
            moved.append(new)
        share = jnp.clip(moved[2], 0.0, 1.0)
        high, low = split_two(share)
        weight_ref[0:GRID, lanes] = jnp.where(mask, 1.0, 0.0).astype(jnp.bfloat16)
        weight_ref[GRID:2 * GRID, lanes] = jnp.where(
            mask, high.astype(jnp.float32), 0.0).astype(jnp.bfloat16)
        weight_ref[2 * GRID:, lanes] = jnp.where(
            mask, low.astype(jnp.float32), 0.0).astype(jnp.bfloat16)

    def one_group(g, first, size):
        for slot in range(group):
            one_bead(g * group + slot, slot, first, size)
        total_ref[:, first:first + size] += lax.dot_general(
            weight_ref[...], hot_ref[0:size, :], (((1,), (1,)), ((), ())),
            preferred_element_type=jnp.float32)

    pl.loop(0, HEAD_BEADS // group)(lambda g: one_group(g, 0, half))
    pl.loop(HEAD_BEADS // group, TAIL_BEAD // group)(lambda g: one_group(g, 0, width))
    pl.loop(TAIL_BEAD // group, beads // group)(lambda g: one_group(g, half, half))

    for species in range(2):
        base = species * half
        upper = None
        for layer in range(layers):
            lanes = slice(base + layer * GRID, base + (layer + 1) * GRID)
            count = total_ref[0:GRID, lanes]
            rise = total_ref[GRID:2 * GRID, lanes] + total_ref[2 * GRID:, lanes]
            lower = count - rise
            sums_ref[species, layer] = lower if upper is None else lower + upper
            upper = rise
        carry_ref[species] = upper

    slots = chosen_ref.shape[1]
    place = jnp.concatenate([place_ref[k] for k in range(3)], axis=0)
    pieces = jnp.concatenate(split_three(place), axis=0)
    bead_of = lax.broadcasted_iota(jnp.int32, (beads, slots), 1) // (slots // beads)
    own = bead_of == lax.broadcasted_iota(jnp.int32, (beads, slots), 0)
    slot_of = lax.broadcasted_iota(jnp.int32, (1, slots), 1) % (slots // beads)
    for way, lift in ((0, -float(layers)), (1, float(layers))):
        hot = lax.broadcasted_iota(jnp.int32, (chains, slots), 0) == chosen_ref[way:way + 1]
        hot = jnp.where(hot, 1.0, 0.0).astype(jnp.bfloat16)
        got = jnp.dot(pieces, hot, preferred_element_type=jnp.float32)
        kept = slot_of < used_ref[way:way + 1]
        for k in range(3):
            part = sum(
                got[(p * 3 + k) * beads:(p * 3 + k + 1) * beads] for p in range(3))
            line = jnp.sum(jnp.where(own, part, 0.0), axis=0, keepdims=True)
            if k == 2:
                line = line + lift
            picked_ref[way, k:k + 1, :] = jnp.where(kept, line, 0.0)


def bead_step(cells, offsets, displacements, block_split, fields, below, above, chosen, used):
    chains = block_split.shape[1]
    beads = cells.shape[1] // chains
    layers = fields.shape[1]
    width = 2 * layers * GRID
    group = 4
    f32 = jnp.float32
    return pl.pallas_call(
        functools.partial(step_kernel, layers, beads, chains),
        out_shape=(
            jax.ShapeDtypeStruct(offsets.shape, f32),
            jax.ShapeDtypeStruct((2, layers, GRID, GRID), f32),
            jax.ShapeDtypeStruct((2, GRID, GRID), f32),
            jax.ShapeDtypeStruct((2, 3, chosen.shape[1]), f32),
        ),
        in_specs=[pl.BlockSpec(memory_space=pltpu.VMEM)] * 9,
        out_specs=[pl.BlockSpec(memory_space=pltpu.VMEM)] * 4,
        scratch_shapes=[
            pltpu.VMEM((6 * GRID, width), jnp.bfloat16),
            pltpu.VMEM((width, group * chains), jnp.bfloat16),
            pltpu.VMEM((3 * GRID, group * chains), jnp.bfloat16),
            pltpu.VMEM((3 * GRID, width), f32),
            pltpu.VMEM((3, beads, chains), f32),
        ],
        compiler_params=pltpu.CompilerParams(vmem_limit_bytes=48 * 1024 * 1024),
        name="bead_step",
    )(cells, offsets, displacements, block_split, fields, below, above, chosen, used)


def shifted(value, axis, steps):
    count = lax.axis_size(axis)
    return lax.ppermute(value, axis, [(i, (i + steps) % count) for i in range(count)])


def shards(cells, offsets, displacements, block_split, fields, crossing, crossing_counts):
    chain_count = block_split.shape[0]
    bead_count = cells.shape[1] // chain_count
    layer_count = fields.shape[1]
    planes = fields.reshape(2, layer_count, GRID, GRID)
    below = shifted(planes[:, -1], "dom", 1)
    above = shifted(planes[:, 0], "dom", -1)
    chosen = jnp.tile(crossing[0], (1, bead_count))
    used = jnp.broadcast_to(crossing_counts[0][:, None], chosen.shape)
    new, sums, carry, picked = bead_step(
        cells, offsets, displacements, block_split[None], planes, below, above, chosen, used)
    carried = shifted(carry, "dom", 1)
    arrived = jnp.stack([shifted(picked[0], "dom", 1), shifted(picked[1], "dom", -1)])
    sums = sums.at[:, 0].add(carried)
    density_sum = lax.psum_scatter(
        sums.reshape(2, layer_count, -1), "rep", scatter_dimension=2, tiled=True)
    density_scale = GRID * GRID * layer_count / (lax.axis_size("rep") * chain_count * bead_count)
    return new, density_sum * density_scale, arrived


def solution(mesh):
    in_specs = (
        P(None, ("dom", "rep")),
        P(None, ("dom", "rep")),
        P(None, ("dom", "rep")),
        P(("dom", "rep")),
        P(None, "dom", None),
        P(("dom", "rep"), None, None),
        P(("dom", "rep"), None),
    )
    out_specs = (P(None, ("dom", "rep")), P(None, "dom", "rep"), P(None, None, ("dom", "rep")))
    return jax.shard_map(shards, mesh=mesh, in_specs=in_specs, out_specs=out_specs, check_vma=False)
```

time: 1090 us -> 912 us (0.84); the launches traced: 1070 us -> 910 us
  local copies, waits for them, and re-layouts: 295 us -> 79.1 us
  waiting for transfers between devices: 547 us -> 744 us
  other arithmetic: 187 us -> 0.67 us
  Pallas kernels: 0 us -> 42.2 us
    unnamed x1 -> x2, waiting for transfers between devices: 0.02 us -> 725 us
    psum x1 -> x0, waiting for transfers between devices: 537 us -> none  [reduce_grid(): summed_all = lax.psum(grid_sum, 'rep')]
    gather x4 -> x0, local copies, waits for them, and re-layouts: 244 us -> none  [the longest x2 243 us: move_beads(): field_push = forces[:, lookup]]
    scatter-add x3 -> x1, other arithmetic: 171 us -> 0.05 us  [shards(): sums = sums.at[:, 0].add(carried)]
    unnamed x43 -> x14, local copies, waits for them, and re-layouts: 5.15 us -> 76.9 us
    pallas_call x0 -> x1, Pallas kernels: none -> 42.2 us  [bead_step(): pl.pallas_call(functools.partial(step_kernel, layers, beads, chains), out...]
    another operation x2, local copies, waits for them, and re-layouts: 35.1 us -> 0.77 us  [shards(): chosen = jnp.tile(crossing[0], (1, bead_count))]
  transfers between devices with their start and end apart: 6 -> 6, of which waited for: 2 -> 4; matrix products, arithmetic and copies ran while one was open for 2% -> 0% of each run, Pallas kernels for 0% -> 0%
where the time goes in v1:
time: 912 us; the launch traced here: 910 us
  waiting for transfers between devices  744 us (82%)
  local copies, waits for them, and re-layouts  79.1 us (9%)
  Pallas kernels  42.2 us (5%)
  starting transfers between devices  30.3 us (3%)
  between operations  14.2 us (2%)
    unnamed x2, waiting for transfers between devices  725 us
    unnamed x14, local copies, waits for them, and re-layouts  76.9 us
    pallas_call x1, Pallas kernels, bead_step(): pl.pallas_call(functools.partial(step_kernel, layers, beads, chains), out...  42.2 us
    ppermute x5, starting transfers between devices, shifted(): lax.ppermute(value, axis, [(i, (i + steps) % count) for i in range(count)])  30.3 us
    ppermute x5, waiting for transfers between devices, shifted(): lax.ppermute(value, axis, [(i, (i + steps) % count) for i in range(count)])  18.9 us
  transfers between devices with their start and end apart: 6, of which 4 were waited for; matrix products, arithmetic and copies ran while one was open for 0% of the time, Pallas kernels for 0%

profile of v1, /device:TPU:1, one launch (start us, length us, event | category | flops | bytes accessed | tf_op | source)
XLA Modules:
  0.0 910.2 jit_solution(1154384305636554302)
XLA Ops:
  7.2 0.0 reduce-scatter.4.cloned.1.call-start
  7.2 1.5 copy.20
  8.7 0.6 reshape.55
  9.3 0.1 slice_bitcast_fusion
  9.4 8.8 collective-permute-start.1
  18.1 1.9 collective-permute-start
  20.1 0.1 copy.21.field_ref
  20.1 0.7 tile.11
  20.8 0.1 tile.12.chosen_ref
  20.9 0.0 collective-permute-done.1.above_ref
  20.9 5.7 collective-permute-done.below_ref
  26.6 0.7 broadcast_in_dim.12.used_ref
  27.3 0.0 copy-start
  27.3 0.9 copy-done
  28.3 0.0 copy-start.1
  28.3 0.9 copy-done.1
  29.2 0.0 copy-start.2
  29.2 0.9 copy-done.2
  30.2 0.0 copy-start.3
  30.2 0.7 copy-done.3
  30.8 42.2 %bead_step.1 = (f32[3,16384]{1,0:T(4,128)}, f32[2,2,192,192]{3,2,1,0:T(8,128)S(1)}, f32[2,192,192]{2,1,0:T(8,128)S(1)}, f32[2,3,512]{2,1,0:T(4,128)S(1)}) custom-call(s32[3,16384]{1,0:T(4,128)S(1)} %copy-done, f32[3,16384]{1,0:T(4,128)S(1)} %copy-done.1, f32[3,16384]{1,0:T(4,128)S(1)} %copy-done.2, s32[1,512]{1,0:T(1,128)S(1)} %bitcast.25, ...), custom_call_target="tpu_custom_call" | custom-call | tf_op jit(solution)/shard_map/bead_step/pallas_call | solution.py:156
  73.0 3.2 collective-permute-start.2
  76.2 0.1 copy.22
  76.2 12.5 %collective-permute-done.2 = f32[2,192,192]{2,1,0:T(8,128)S(1)} collective-permute-done((f32[2,192,192]{2,1,0:T(8,128)S(1)}, f32[2,192,192]{2,1,0:T(8,128)S(1)}, u32[]{:S(2)}, u32[]{:S(2)}) %collective-permute-start.2) | collective-permute-done | bytes 294944 | tf_op jit(solution)/shard_map/ppermute | solution.py:180
  88.7 0.1 fusion.1
  88.8 33.3 %copy.27 = f32[2,2,192,192]{1,0,3,2:T(2,128)} copy(f32[2,2,192,192]{3,2,1,0:T(8,128)S(1)} %fusion.1) | data formatting | bytes 1179648
  122.1 35.1 %reshape.58 = f32[36864,4]{1,0:T(8,128)} reshape(f32[36864,2,2]{2,1,0:T(2,128)} %bitcast.26) | data formatting | bytes 1179648
  157.2 0.0 reduce-scatter.4.cloned.1.call-update
  157.3 1.9 collective-permute-start.3
  159.2 14.5 %collective-permute-start.4 = (f32[3,512]{1,0:T(4,128)S(1)}, f32[3,512]{1,0:T(4,128)S(1)}, u32[]{:S(2)}, u32[]{:S(2)}) collective-permute-start(f32[3,512]{1,0:T(4,128)S(1)} %get-tuple-element.35), channel_id=1, source_target_pairs={{0,480},{32,0},{64,32},{96,64},{128,96},{160,128},{192,160},{224,1... | collective-permute-start | bytes 18440 | tf_op jit(solution)/shard_map/ppermute | solution.py:180
  173.7 0.0 collective-permute-done.3
  173.7 0.8 collective-permute-done.4
  174.5 0.6 copy.24
  175.1 724.9 %reduce-scatter.4.cloned.1.call-done = f32[1152,4]{1,0:T(8,128)} async-done(((f32[36864,4]{1,0:T(8,128)}), f32[1152,4]{1,0:T(8,128)}) %reduce-scatter.4.cloned.1.call-update) | async-done | bytes 18448
  900.0 1.7 reshape.59
  901.8 1.0 copy.26
  902.8 0.6 broadcast_multiply_fusion
  (2 shorter events, 0.0 us)
Async XLA Ops:
  7.2 892.9 %reduce-scatter.4.cloned.1.call-start = ((), (), s32[]{:S(2)}) async-start(), calls=%async_computation.1 | async-start | bytes 19464192
  9.4 11.6 %collective-permute-start.1 = (f32[2,192,192]{2,1,0:T(8,128)S(1)}, f32[2,192,192]{2,1,0:T(8,128)S(1)}, u32[]{:S(2)}, u32[]{:S(2)}) collective-permute-start(f32[2,192,192]{2,1,0:T(8,128)S(1)} %get-tuple-element.32), channel_id=1, source_target_pairs={{0,480},{32,0},{64,32},{96,64},{128,96},{160,128},{192,160},{224,1... | collective-permute-start | bytes 884744 | tf_op jit(solution)/shard_map/ppermute | solution.py:180
  18.1 8.4 collective-permute-start
  27.3 0.9 copy-start
  28.3 0.9 copy-start.1
  29.2 0.9 copy-start.2
  30.2 0.7 copy-start.3
  73.0 15.7 %collective-permute-start.2 = (f32[2,192,192]{2,1,0:T(8,128)S(1)}, f32[2,192,192]{2,1,0:T(8,128)S(1)}, u32[]{:S(2)}, u32[]{:S(2)}) collective-permute-start(f32[2,192,192]{2,1,0:T(8,128)S(1)} %get-tuple-element.21), channel_id=1, source_target_pairs={{0,32},{32,64},{64,96},{96,128},{128,160},{160,192},{192,224},{224... | collective-permute-start | bytes 884744 | tf_op jit(solution)/shard_map/ppermute | solution.py:180
  157.3 16.4 %collective-permute-start.3 = (f32[3,512]{1,0:T(4,128)S(1)}, f32[3,512]{1,0:T(4,128)S(1)}, u32[]{:S(2)}, u32[]{:S(2)}) collective-permute-start(f32[3,512]{1,0:T(4,128)S(1)} %get-tuple-element.34), channel_id=1, source_target_pairs={{0,32},{32,64},{64,96},{96,128},{128,160},{160,192},{192,224},{224... | collective-permute-start | bytes 18440 | tf_op jit(solution)/shard_map/ppermute | solution.py:180
  159.2 15.3 %collective-permute-start.4 = (f32[3,512]{1,0:T(4,128)S(1)}, f32[3,512]{1,0:T(4,128)S(1)}, u32[]{:S(2)}, u32[]{:S(2)}) collective-permute-start(f32[3,512]{1,0:T(4,128)S(1)} %get-tuple-element.35), channel_id=1, source_target_pairs={{0,480},{32,0},{64,32},{96,64},{128,96},{160,128},{192,160},{224,1... | collective-permute-start | bytes 18440 | tf_op jit(solution)/shard_map/ppermute | solution.py:180
Sparse Core Ops, SparseCore 0:
  157.4 742.6 reduce-scatter.3

commit v2 on v1

v2 whole, which is shorter than its diff:
```python
import functools

import jax
import jax.numpy as jnp
from jax import lax
from jax.experimental import pallas as pl
from jax.experimental.pallas import tpu as pltpu
from jax.sharding import PartitionSpec as P

GRID = 192
CELLS = GRID * GRID
LANES = 128
ROWS = CELLS // LANES
MOBILITY = 0.1
HEAD_BEADS = 8
TAIL_BEAD = 24
GROUP = 4
EARLY_BEADS = 8
VMEM_BYTES = 56 * 1024 * 1024
F32 = jnp.float32
BF16 = jnp.bfloat16


E4 = jnp.float8_e4m3fn
PIECES = 3
FORCE_SCALE = 32.0
SHARE_SCALE = 256.0


def split_e4(value):
    pieces = []
    for _ in range(PIECES):
        pieces.append(value.astype(E4))
        value = value - pieces[-1].astype(F32)
    return pieces


def split_three(value):
    high = value.astype(BF16)
    rest = value - high.astype(F32)
    mid = rest.astype(BF16)
    low = (rest - mid.astype(F32)).astype(BF16)
    return high, mid, low


def wrap_gap(gap):
    gap = jnp.where(gap >= GRID // 2, gap - GRID, gap)
    return jnp.where(gap < -(GRID // 2), gap + GRID, gap)


def ahead(plane, steps):
    rows, lanes = divmod(steps % CELLS, LANES)

    def rolled(count):
        count %= ROWS
        return jnp.concatenate([plane[count:], plane[:count]], axis=0) if count else plane

    if lanes == 0:
        return rolled(rows)
    lane = lax.broadcasted_iota(jnp.int32, plane.shape, 1)
    return pltpu.roll(jnp.where(lane >= lanes, rolled(rows), rolled(rows + 1)), LANES - lanes, 1)


def force_x(plane):
    return (ahead(plane, -GRID) - ahead(plane, GRID)) * 0.5


def force_y(plane):
    cell = lax.broadcasted_iota(jnp.int32, plane.shape, 0) * LANES
    y = lax.rem(cell + lax.broadcasted_iota(jnp.int32, plane.shape, 1), GRID)
    back = jnp.where(y == 0, ahead(plane, GRID - 1), ahead(plane, -1))
    fore = jnp.where(y == GRID - 1, ahead(plane, 1 - GRID), ahead(plane, 1))
    return (back - fore) * 0.5


def one_hot_e4(rows, key):
    return jnp.concatenate([
        jnp.where(block, jnp.ones((), E4), jnp.zeros((), E4)) for block in masks_e4(rows, key)], axis=0)


def masks_e4(rows, key):
    step = 128 if rows % 128 == 0 else 96
    lane = lax.broadcasted_iota(jnp.int8, (step, key.shape[1]), 0)
    masks = []
    for start in range(0, rows, step):
        local = key - start
        local = jnp.where((local >= 0) & (local < step), local, -1).astype(jnp.int8)
        masks.append(lane == local)
    return masks


def bead_row(ref, k, bead, chains):
    return ref[k:k + 1, pl.ds(pl.multiple_of(bead * chains, chains), chains)]


def bead_keys(cells_ref, split_ref, j, chains, layers, whole):
    cell = bead_row(cells_ref, 0, j, chains) * GRID + bead_row(cells_ref, 1, j, chains)
    column = bead_row(cells_ref, 2, j, chains) * LANES + (cell & (LANES - 1))
    if whole:
        column = column + jnp.where(j >= split_ref[...], layers * LANES, 0)
    return cell >> 7, column


def new_row(cells_ref, offsets_ref, displace_ref, k, j, push, chains, beads):
    before, after = jnp.maximum(j - 1, 0), jnp.minimum(j + 1, beads - 1)
    row = functools.partial(bead_row, chains=chains)
    cell, off = row(cells_ref, k, j), row(offsets_ref, k, j)
    gap_after = row(cells_ref, k, after) - cell
    gap_before = cell - row(cells_ref, k, before)
    if k < 2:
        gap_after, gap_before = wrap_gap(gap_after), wrap_gap(gap_before)
    gap_after = gap_after.astype(F32) + (row(offsets_ref, k, after) - off)
    gap_before = gap_before.astype(F32) + (off - row(offsets_ref, k, before))
    return off + MOBILITY * ((gap_after - gap_before) + push) + row(displace_ref, k, j)


def over_beads(body, start, stop, layers):
    half = layers * LANES
    for low, high, first, size in (
        (0, HEAD_BEADS, 0, half), (HEAD_BEADS, TAIL_BEAD, 0, 2 * half), (TAIL_BEAD, stop, half, half),
    ):
        low, high = max(low, start), min(high, stop)
        if low < high:
            pl.loop(low // GROUP, high // GROUP)(functools.partial(body, first=first, size=size))


def gather(table_ref, hot, first, parts, row):
    size, chains = hot.shape
    width = table_ref.shape[1] // PIECES
    rows = sum(
        jnp.dot(table_ref[:, p * width + first:p * width + first + size], hot, preferred_element_type=F32)
        for p in range(PIECES))
    sub = lax.broadcasted_iota(jnp.int32, (8, chains), 0)
    found = [jnp.zeros((8, chains), F32)] * parts
    for start in range(0, ROWS, 8):
        mask = sub + start == row
        for k in range(parts):
            found[k] = jnp.where(mask, rows[k * ROWS + start:k * ROWS + start + 8], found[k])
    return [jnp.sum(part, axis=0, keepdims=True) * (1 / FORCE_SCALE) for part in found]


def plane_beads(start, stop, layers, beads, chains, cells_ref, offsets_ref, displace_ref, split_ref,
                table_ref, new_ref):
    width = 2 * layers * LANES

    def body(g, first, size):
        for slot in range(GROUP):
            j = g * GROUP + slot
            row, column = bead_keys(cells_ref, split_ref, j, chains, layers, size == width)
            for k, push in enumerate(gather(table_ref, one_hot_e4(size, column), first, 2, row)):
                new_ref[k:k + 1, pl.ds(pl.multiple_of(j * chains, chains), chains)] = new_row(
                    cells_ref, offsets_ref, displace_ref, k, j, push, chains, beads)

    over_beads(body, start, stop, layers)


def early_kernel(layers, beads, chains, cells_ref, offsets_ref, displace_ref, split_ref, field_ref,
                 flat_ref, table_ref):
    width = 2 * layers * LANES
    for species in range(2):
        for layer in range(layers):
            plane = field_ref[species, layer]
            at = (species * layers + layer) * LANES
            for k, force in enumerate((force_x, force_y)):
                for p, piece in enumerate(split_e4(force(plane) * FORCE_SCALE)):
                    table_ref[k * ROWS:(k + 1) * ROWS, p * width + at:p * width + at + LANES] = piece
    plane_beads(0, EARLY_BEADS, layers, beads, chains, cells_ref, offsets_ref, displace_ref, split_ref,
                table_ref, flat_ref)


def late_kernel(layers, beads, chains, cells_ref, offsets_ref, displace_ref, split_ref, flat_ref,
                table_ref, rise_ref, chosen_ref, used_ref, new_ref, picked_ref, place_ref):
    new_ref[0:2, 0:EARLY_BEADS * chains] = flat_ref[...]
    new_ref[2:3, :] = rise_ref[...]
    plane_beads(EARLY_BEADS, beads, layers, beads, chains, cells_ref, offsets_ref, displace_ref, split_ref,
                table_ref, new_ref)

    for k in range(3):
        for j in range(beads):
            place_ref[k * beads + j:k * beads + j + 1, :] = (
                bead_row(cells_ref, k, j, chains).astype(F32) + bead_row(new_ref, k, j, chains))
    slots = chosen_ref.shape[1]
    pieces = jnp.concatenate(split_three(place_ref[...]), axis=0)
    bead_of = lax.broadcasted_iota(jnp.int32, (beads, slots), 1) // (slots // beads)
    own = bead_of == lax.broadcasted_iota(jnp.int32, (beads, slots), 0)
    slot_of = lax.broadcasted_iota(jnp.int32, (1, slots), 1) % (slots // beads)
    for way, lift in ((0, -float(layers)), (1, float(layers))):
        hot = lax.broadcasted_iota(jnp.int32, (chains, slots), 0) == chosen_ref[way:way + 1]
        hot = jnp.where(hot, 1.0, 0.0).astype(BF16)
        got = jnp.dot(pieces, hot, preferred_element_type=F32)
        kept = slot_of < used_ref[way:way + 1]
        for k in range(3):
            part = sum(got[(p * 3 + k) * beads:(p * 3 + k + 1) * beads] for p in range(3))
            line = jnp.sum(jnp.where(own, part, 0.0), axis=0, keepdims=True)
            if k == 2:
                line = line + lift
            picked_ref[way, k:k + 1, :] = jnp.where(kept, line, 0.0)


def rise_kernel(layers, beads, chains, cells_ref, offsets_ref, displace_ref, split_ref, field_ref,
                below_ref, above_ref, rise_ref, sums_ref, carry_ref,
                table_ref, hot_ref, weight_ref, total_ref):
    width = 2 * layers * LANES
    for species in range(2):
        stack = [below_ref[species]] + [field_ref[species, k] for k in range(layers)] + [above_ref[species]]
        for layer in range(layers):
            at = (species * layers + layer) * LANES
            force = (stack[layer] - stack[layer + 2]) * (0.5 * FORCE_SCALE)
            for p, piece in enumerate(split_e4(force)):
                table_ref[:, p * width + at:p * width + at + LANES] = piece
    total_ref[...] = jnp.zeros_like(total_ref)

    def body(g, first, size):
        for slot in range(GROUP):
            j = g * GROUP + slot
            lanes = slice(slot * chains, (slot + 1) * chains)
            row, column = bead_keys(cells_ref, split_ref, j, chains, layers, size == width)
            hot = one_hot_e4(size, column)
            hot_ref[0:size, lanes] = hot
            push, = gather(table_ref, hot, first, 1, row)
            new = new_row(cells_ref, offsets_ref, displace_ref, 2, j, push, chains, beads)
            rise_ref[0:1, pl.ds(pl.multiple_of(j * chains, chains), chains)] = new
            pieces = [jnp.ones(new.shape, E4)] + split_e4(jnp.clip(new, 0.0, 1.0) * SHARE_SCALE)
            for b, block in enumerate(masks_e4(ROWS, row)):
                step = block.shape[0]
                for p, piece in enumerate(pieces):
                    weight_ref[p * ROWS + b * step:p * ROWS + (b + 1) * step, lanes] = jnp.where(
                        block, jnp.broadcast_to(piece, block.shape), jnp.zeros((), E4))
        total_ref[:, first:first + size] += lax.dot_general(
            weight_ref[...], hot_ref[0:size, :], (((1,), (1,)), ((), ())), preferred_element_type=F32)

    over_beads(body, 0, beads, layers)

    shares, _, share = sums_ref.shape
    per = share // LANES

    def place(ref, slab, value):
        for r in range(shares):
            for n in range(per):
                ref[r, slab:slab + 1, n * LANES:(n + 1) * LANES] = value[r * per + n:r * per + n + 1]

    for species in range(2):
        upper = None
        for layer in range(layers):
            at = (species * layers + layer) * LANES
            count, *rises = (total_ref[p * ROWS:(p + 1) * ROWS, at:at + LANES] for p in range(1 + PIECES))
            rise = sum(rises) * (1 / SHARE_SCALE)
            place(sums_ref, layer * 2 + species, count - rise if upper is None else count - rise + upper)
            upper = rise
        place(carry_ref, species, upper)


def local_call(kernel, name, shapes, scratch, operands):
    return pl.pallas_call(
        kernel,
        out_shape=tuple(jax.ShapeDtypeStruct(shape, dtype) for shape, dtype in shapes),
        in_specs=[pl.BlockSpec(memory_space=pltpu.VMEM)] * len(operands),
        out_specs=tuple([pl.BlockSpec(memory_space=pltpu.VMEM)] * len(shapes)),
        scratch_shapes=[pltpu.VMEM(shape, dtype) for shape, dtype in scratch],
        compiler_params=pltpu.CompilerParams(vmem_limit_bytes=VMEM_BYTES),
        name=name,
    )(*operands)


def ring(value, steps):
    doms, reps = lax.axis_size("dom"), lax.axis_size("rep")
    pairs = []
    for dom in range(doms):
        for rep in range(reps):
            turn = reps // 8 if not 0 <= dom + steps < doms else 0
            pairs.append((dom * reps + rep, (dom + steps) % doms * reps + (rep ^ turn)))
    return lax.ppermute(value, ("dom", "rep"), pairs)


def shifted(value, axis, steps):
    count = lax.axis_size(axis)
    return lax.ppermute(value, axis, [(i, (i + steps) % count) for i in range(count)])


def shards(cells, offsets, displacements, block_split, fields, crossing, crossing_counts):
    chains = block_split.shape[0]
    beads = cells.shape[1] // chains
    layers = fields.shape[1]
    shares = lax.axis_size("rep")
    width = 2 * layers * LANES
    sizes = (layers, beads, chains)
    planes = fields.reshape(2, layers, ROWS, LANES)
    chosen = jnp.tile(crossing[0], (1, beads))
    used = jnp.broadcast_to(crossing_counts[0][:, None], chosen.shape)
    beads_in = (cells, offsets, displacements, block_split[None])

    below = ring(planes[:, -1], 1)
    above = ring(planes[:, 0], -1)
    flat, table = local_call(
        functools.partial(early_kernel, *sizes), "early_step",
        (((2, EARLY_BEADS * chains), F32), ((2 * ROWS, PIECES * width), E4)), (), (*beads_in, planes))
    below, above, flat = lax.optimization_barrier((below, above, flat))
    rise, sums, carry = local_call(
        functools.partial(rise_kernel, *sizes), "rise_step",
        (((1, beads * chains), F32), ((shares, 2 * layers, CELLS // shares), F32),
         ((shares, 2, CELLS // shares), F32)),
        (((ROWS, PIECES * width), E4), ((width, GROUP * chains), E4),
         (((1 + PIECES) * ROWS, GROUP * chains), E4), (((1 + PIECES) * ROWS, width), F32)),
        (*beads_in, planes, below, above))
    carried = ring(carry, 1)
    sums = sums + jnp.pad(carried, ((0, 0), (0, 2 * layers - 2), (0, 0)))
    sums, rise = lax.optimization_barrier((sums, rise))
    parts = lax.all_to_all(sums, "rep", split_axis=0, concat_axis=0, tiled=True)
    new, picked = local_call(
        functools.partial(late_kernel, *sizes), "late_step",
        (((3, beads * chains), F32), ((2, 3, chosen.shape[1]), F32)),
        (((3 * beads, chains), F32),), (*beads_in, flat, table, rise, chosen, used))
    arrived = jnp.stack([shifted(picked[0], "dom", 1), shifted(picked[1], "dom", -1)])
    density_scale = GRID * GRID * layers / (shares * chains * beads)
    density = jnp.sum(parts, axis=0) * density_scale
    return new, density.reshape(layers, 2, -1).transpose(1, 0, 2), arrived


def solution(mesh):
    in_specs = (
        P(None, ("dom", "rep")),
        P(None, ("dom", "rep")),
        P(None, ("dom", "rep")),
        P(("dom", "rep")),
        P(None, "dom", None),
        P(("dom", "rep"), None, None),
        P(("dom", "rep"), None),
    )
    out_specs = (P(None, ("dom", "rep")), P(None, "dom", "rep"), P(None, None, ("dom", "rep")))
    return jax.shard_map(shards, mesh=mesh, in_specs=in_specs, out_specs=out_specs, check_vma=False)
```

time: 912 us -> 99 us (0.11)
  the two profiles are of different devices: /device:TPU:1 before, /device:TPU:32 now
where the time goes in v2:
time: 99 us; the launch traced here: 98.5 us
  Pallas kernels  40 us (40%)
  starting transfers between devices  24.4 us (25%)
  waiting for transfers between devices  23.4 us (24%)
  local copies, waits for them, and re-layouts  7.84 us (8%)
  other arithmetic  2.16 us (2%)
    pallas_call x3, Pallas kernels, local_call(): pl.pallas_call(kernel, out_shape=tuple((jax.ShapeDtypeStruct(shape, dtype...  40 us
    all_to_all x1, starting transfers between devices, shards(): parts = lax.all_to_all(sums, 'rep', split_axis=0, concat_axis=0, tiled=True)  17.7 us
    ppermute x2, waiting for transfers between devices, shifted(): lax.ppermute(value, axis, [(i, (i + steps) % count) for i in range(count)])  9.71 us
    ppermute x3, waiting for transfers between devices, ring(): return lax.ppermute(value, ('dom', 'rep'), pairs)  7.89 us
    all_to_all x1, waiting for transfers between devices, shards(): parts = lax.all_to_all(sums, 'rep', split_axis=0, concat_axis=0, tiled=True)  5.75 us
    ppermute x2, starting transfers between devices, shifted(): lax.ppermute(value, axis, [(i, (i + steps) % count) for i in range(count)])  4.31 us
    unnamed x12, local copies, waits for them, and re-layouts  4.15 us
    ppermute x3, starting transfers between devices, ring(): return lax.ppermute(value, ('dom', 'rep'), pairs)  2.33 us
  transfers between devices with their start and end apart: 6, of which 4 were waited for; matrix products, arithmetic and copies ran while one was open for 3% of the time, Pallas kernels for 20%

profile of v2, /device:TPU:32, one launch (start us, length us, event | category | flops | bytes accessed | tf_op | source)
XLA Modules:
  0.0 98.5 jit_solution(3326171470080174091)
XLA Ops:
  0.6 1.6 %reshape.19.field_ref = f32[2,2,288,128]{3,2,1,0:T(8,128)S(1)} reshape(f32[2,2,36864]{2,1,0:T(2,128)} %param.11) | data formatting | bytes 1179648 | tf_op jit(solution)/shard_map/reshape | solution.py:287
  2.2 0.0 copy-start
  2.3 0.8 copy-done
  3.0 0.0 collective-permute-start
  3.0 1.7 %collective-permute-start.1 = (f32[2,288,128]{2,1,0:T(8,128)S(1)}, f32[2,288,128]{2,1,0:T(8,128)S(1)}, u32[]{:S(2)}, u32[]{:S(2)}) collective-permute-start(f32[2,288,128]{2,1,0:T(8,128)S(1)} %get-tuple-element.33), channel_id=1, source_target_pairs={{0,484},{1,485},{2,486},{3,487},{4,480},{5,481},{6,482},{7,483},{8... | collective-permute-start | bytes 884744 | tf_op jit(solution)/shard_map/ppermute | solution.py:272
  4.8 5.7 %early_step.1 = (f32[2,4096]{1,0:T(2,128)}, f8e4m3fn[576,1536]{1,0:T(32,128)(4,1)}) custom-call(s32[3,16384]{1,0:T(4,128)} %cells_ref.5, f32[3,16384]{1,0:T(4,128)} %offsets_ref.5, f32[3,16384]{1,0:T(4,128)} %displace_ref.5, s32[1,512]{1,0:T(1,128)} %bitcast.19, f32[2,2,288,128]{3,2,1,0:T(8,128)} %copy-done), custom_call_target="tpu_custom_call" | custom-call | tf_op jit(solution)/shard_map/early_step/pallas_call | solution.py:254
  10.5 0.0 collective-permute-done.below_ref
  10.5 0.0 copy-start.1
  10.5 0.0 collective-permute-done.1.above_ref
  10.5 0.0 copy-start.2
  10.5 0.7 copy-done.1
  11.2 0.1 copy-done.2
  11.4 20.2 %rise_step.1 = (f32[1,16384]{1,0:T(1,128)}, f32[32,4,1152]{2,1,0:T(4,128)}, f32[32,2,1152]{2,1,0:T(2,128)}) custom-call(s32[3,16384]{1,0:T(4,128)} %cells_ref.5, f32[3,16384]{1,0:T(4,128)} %offsets_ref.5, f32[3,16384]{1,0:T(4,128)} %displace_ref.5, s32[1,512]{1,0:T(1,128)} %bitcast.20, f32[2,2,288,128]{3,2,1,0:T(8,128)} %copy-done, ...), custom_call_target="tpu_custom_call" | custom-call | tf_op jit(solution)/shard_map/rise_step/pallas_call | solution.py:254
  31.6 0.6 collective-permute-start.2
  32.1 7.9 %collective-permute-done.2 = f32[32,2,1152]{2,1,0:T(2,128)S(1)} collective-permute-done((f32[32,2,1152]{2,1,0:T(2,128)}, f32[32,2,1152]{2,1,0:T(2,128)S(1)}, u32[]{:S(2)}, u32[]{:S(2)}) %collective-permute-start.2) | collective-permute-done | bytes 294944 | tf_op jit(solution)/shard_map/ppermute | solution.py:272
  40.0 2.0 %pad_add_fusion = f32[32,4,1152]{2,1,0:T(4,128)} fusion(f32[32,4,1152]{2,1,0:T(4,128)} %get-tuple-element.20, f32[32,2,1152]{2,1,0:T(2,128)S(1)} %collective-permute-done.2), kind=kLoop, calls=%fused_computation | loop fusion | flops 147456 | bytes 1474560 | tf_op jit(solution)/shard_map/add | solution.py:306
  42.1 17.7 %all-to-all-start = ((f32[32,4,1152]{2,1,0:T(4,128)}), f32[32,4,1152]{2,1,0:T(4,128)S(1)}, u32[]{:S(2)}, u32[]{:S(2)}) async-start(f32[32,4,1152]{2,1,0:T(4,128)} %pad_add_fusion), calls=%async_computation | async-start | bytes 1179648 | tf_op jit(solution)/shard_map/all_to_all | solution.py:308
  59.8 0.0 copy-start.3
  59.8 0.7 copy-done.3
  60.5 0.7 tile.12.chosen_ref
  61.2 0.0 copy-start.4
  61.2 0.7 copy-done.4
  61.8 0.7 broadcast_in_dim.12.used_ref
  62.5 14.1 %late_step.1 = (f32[3,16384]{1,0:T(4,128)}, f32[2,3,512]{2,1,0:T(4,128)}) custom-call(s32[3,16384]{1,0:T(4,128)} %cells_ref.5, f32[3,16384]{1,0:T(4,128)} %offsets_ref.5, f32[3,16384]{1,0:T(4,128)} %displace_ref.5, s32[1,512]{1,0:T(1,128)} %bitcast.21, f32[2,4096]{1,0:T(2,128)} %get-tuple-element.16.flat_ref, ...), custom_call_target="tpu_custom_call" | custom-call | tf_op jit(solution)/shard_map/late_step/pallas_call | solution.py:254
  76.6 0.7 slice_bitcast_fusion.3
  77.3 1.9 %collective-permute-start.4 = (f32[3,512]{1,0:T(4,128)S(1)}, f32[3,512]{1,0:T(4,128)S(1)}, u32[]{:S(2)}, u32[]{:S(2)}) collective-permute-start(f32[3,512]{1,0:T(4,128)S(1)} %get-tuple-element.36), channel_id=1, source_target_pairs={{0,480},{32,0},{64,32},{96,64},{128,96},{160,128},{192,160},{224,1... | collective-permute-start | bytes 18440 | tf_op jit(solution)/shard_map/ppermute | solution.py:277
  79.3 2.4 %collective-permute-start.3 = (f32[3,512]{1,0:T(4,128)S(1)}, f32[3,512]{1,0:T(4,128)S(1)}, u32[]{:S(2)}, u32[]{:S(2)}) collective-permute-start(f32[3,512]{1,0:T(4,128)S(1)} %get-tuple-element.35), channel_id=1, source_target_pairs={{0,32},{32,64},{64,96},{96,128},{128,160},{160,192},{192,224},{224... | collective-permute-start | bytes 18440 | tf_op jit(solution)/shard_map/ppermute | solution.py:277
  81.7 2.4 %collective-permute-done.4 = f32[3,512]{1,0:T(4,128)S(1)} collective-permute-done((f32[3,512]{1,0:T(4,128)S(1)}, f32[3,512]{1,0:T(4,128)S(1)}, u32[]{:S(2)}, u32[]{:S(2)}) %collective-permute-start.4) | collective-permute-done | bytes 6176 | tf_op jit(solution)/shard_map/ppermute | solution.py:277
  84.1 7.3 %collective-permute-done.3 = f32[3,512]{1,0:T(4,128)S(1)} collective-permute-done((f32[3,512]{1,0:T(4,128)S(1)}, f32[3,512]{1,0:T(4,128)S(1)}, u32[]{:S(2)}, u32[]{:S(2)}) %collective-permute-start.3) | collective-permute-done | bytes 6176 | tf_op jit(solution)/shard_map/ppermute | solution.py:277
  91.4 0.6 copy.18
  92.0 5.8 %all-to-all-done = f32[32,4,1152]{2,1,0:T(4,128)S(1)} async-done(((f32[32,4,1152]{2,1,0:T(4,128)}), f32[32,4,1152]{2,1,0:T(4,128)S(1)}, u32[]{:S(2)}, u32[]{:S(2)}) %all-to-all-start) | async-done | bytes 589856 | tf_op jit(solution)/shard_map/all_to_all | solution.py:308
  97.8 0.1 reduce_sum.9
  97.9 0.6 copy.17
  (5 shorter events, 0.1 us)
Async XLA Ops:
  2.2 0.8 copy-start
  3.0 7.5 %collective-permute-start = (f32[2,288,128]{2,1,0:T(8,128)S(1)}, f32[2,288,128]{2,1,0:T(8,128)S(1)}, u32[]{:S(2)}, u32[]{:S(2)}) collective-permute-start(f32[2,288,128]{2,1,0:T(8,128)S(1)} %get-tuple-element.34), channel_id=1, source_target_pairs={{0,32},{1,33},{2,34},{3,35},{4,36},{5,37},{6,38},{7,39},{8,40},{9,... | collective-permute-start | bytes 884744 | tf_op jit(solution)/shard_map/ppermute | solution.py:272
  3.0 7.5 %collective-permute-start.1 = (f32[2,288,128]{2,1,0:T(8,128)S(1)}, f32[2,288,128]{2,1,0:T(8,128)S(1)}, u32[]{:S(2)}, u32[]{:S(2)}) collective-permute-start(f32[2,288,128]{2,1,0:T(8,128)S(1)} %get-tuple-element.33), channel_id=1, source_target_pairs={{0,484},{1,485},{2,486},{3,487},{4,480},{5,481},{6,482},{7,483},{8... | collective-permute-start | bytes 884744 | tf_op jit(solution)/shard_map/ppermute | solution.py:272
  10.5 0.7 copy-start.1
  10.5 0.8 copy-start.2
  31.6 8.5 %collective-permute-start.2 = (f32[32,2,1152]{2,1,0:T(2,128)}, f32[32,2,1152]{2,1,0:T(2,128)S(1)}, u32[]{:S(2)}, u32[]{:S(2)}) collective-permute-start(f32[32,2,1152]{2,1,0:T(2,128)} %get-tuple-element.21), channel_id=1, source_target_pairs={{0,32},{1,33},{2,34},{3,35},{4,36},{5,37},{6,38},{7,39},{8,40},{9,... | collective-permute-start | bytes 884744 | tf_op jit(solution)/shard_map/ppermute | solution.py:272
  42.1 55.7 %all-to-all-start = ((f32[32,4,1152]{2,1,0:T(4,128)}), f32[32,4,1152]{2,1,0:T(4,128)S(1)}, u32[]{:S(2)}, u32[]{:S(2)}) async-start(f32[32,4,1152]{2,1,0:T(4,128)} %pad_add_fusion), calls=%async_computation | async-start | bytes 1179648 | tf_op jit(solution)/shard_map/all_to_all | solution.py:308
  59.8 0.7 copy-start.3
  61.2 0.7 copy-start.4
  77.3 6.7 %collective-permute-start.4 = (f32[3,512]{1,0:T(4,128)S(1)}, f32[3,512]{1,0:T(4,128)S(1)}, u32[]{:S(2)}, u32[]{:S(2)}) collective-permute-start(f32[3,512]{1,0:T(4,128)S(1)} %get-tuple-element.36), channel_id=1, source_target_pairs={{0,480},{32,0},{64,32},{96,64},{128,96},{160,128},{192,160},{224,1... | collective-permute-start | bytes 18440 | tf_op jit(solution)/shard_map/ppermute | solution.py:277
  79.3 12.1 %collective-permute-start.3 = (f32[3,512]{1,0:T(4,128)S(1)}, f32[3,512]{1,0:T(4,128)S(1)}, u32[]{:S(2)}, u32[]{:S(2)}) collective-permute-start(f32[3,512]{1,0:T(4,128)S(1)} %get-tuple-element.35), channel_id=1, source_target_pairs={{0,32},{32,64},{64,96},{96,128},{128,160},{160,192},{192,224},{224... | collective-permute-start | bytes 18440 | tf_op jit(solution)/shard_map/ppermute | solution.py:277

commit v3 on v2

v3 whole, which is shorter than its diff:
```python
import functools

import jax
import jax.numpy as jnp
from jax import lax
from jax.experimental import pallas as pl
from jax.experimental.pallas import tpu as pltpu
from jax.sharding import PartitionSpec as P

GRID = 192
CELLS = GRID * GRID
LANES = 128
ROWS = CELLS // LANES
MOBILITY = 0.1
HEAD_BEADS = 8
TAIL_BEAD = 24
GROUP = 4
FIRST_BEADS = 20
F32 = jnp.float32
BF16 = jnp.bfloat16


E4 = jnp.float8_e4m3fn
PIECES = 3
FORCE_SCALE = 32.0
SHARE_SCALE = 256.0


def split_e4(value):
    pieces = []
    for _ in range(PIECES):
        pieces.append(value.astype(E4))
        value = value - pieces[-1].astype(F32)
    return pieces


def split_three(value):
    high = value.astype(BF16)
    rest = value - high.astype(F32)
    mid = rest.astype(BF16)
    low = (rest - mid.astype(F32)).astype(BF16)
    return high, mid, low


def wrap_gap(gap):
    gap = jnp.where(gap >= GRID // 2, gap - GRID, gap)
    return jnp.where(gap < -(GRID // 2), gap + GRID, gap)


def ahead(plane, steps):
    rows, lanes = divmod(steps % CELLS, LANES)

    def rolled(count):
        count %= ROWS
        return jnp.concatenate([plane[count:], plane[:count]], axis=0) if count else plane

    if lanes == 0:
        return rolled(rows)
    lane = lax.broadcasted_iota(jnp.int32, plane.shape, 1)
    return pltpu.roll(jnp.where(lane >= lanes, rolled(rows), rolled(rows + 1)), LANES - lanes, 1)


def force_x(plane):
    return (ahead(plane, -GRID) - ahead(plane, GRID)) * 0.5


def force_y(plane):
    cell = lax.broadcasted_iota(jnp.int32, plane.shape, 0) * LANES
    y = lax.rem(cell + lax.broadcasted_iota(jnp.int32, plane.shape, 1), GRID)
    back = jnp.where(y == 0, ahead(plane, GRID - 1), ahead(plane, -1))
    fore = jnp.where(y == GRID - 1, ahead(plane, 1 - GRID), ahead(plane, 1))
    return (back - fore) * 0.5


def one_hot_e4(rows, key):
    return jnp.concatenate([
        jnp.where(block, jnp.ones((), E4), jnp.zeros((), E4)) for block in masks_e4(rows, key)], axis=0)


def masks_e4(rows, key):
    step = 128 if rows % 128 == 0 else 96
    lane = lax.broadcasted_iota(jnp.int8, (step, key.shape[1]), 0)
    masks = []
    for start in range(0, rows, step):
        local = key - start
        local = jnp.where((local >= 0) & (local < step), local, -1).astype(jnp.int8)
        masks.append(lane == local)
    return masks


def bead_row(ref, k, bead, chains):
    return ref[k:k + 1, pl.ds(pl.multiple_of(bead * chains, chains), chains)]


def key_row(x, y, z):
    cell = x * GRID + y
    return cell >> 7, z * LANES + (cell & (LANES - 1))


def bead_keys(cells_ref, split_ref, j, chains, layers, whole):
    row, column = key_row(*(bead_row(cells_ref, k, j, chains) for k in range(3)))
    if whole:
        column = column + jnp.where(j >= split_ref[...], layers * LANES, 0)
    return row, column


def base_row(cells_ref, offsets_ref, displace_ref, k, j, chains, beads):
    before, after = jnp.maximum(j - 1, 0), jnp.minimum(j + 1, beads - 1)
    row = functools.partial(bead_row, chains=chains)
    cell, off = row(cells_ref, k, j), row(offsets_ref, k, j)
    gap_after = row(cells_ref, k, after) - cell
    gap_before = cell - row(cells_ref, k, before)
    if k < 2:
        gap_after, gap_before = wrap_gap(gap_after), wrap_gap(gap_before)
    gap_after = gap_after.astype(F32) + (row(offsets_ref, k, after) - off)
    gap_before = gap_before.astype(F32) + (off - row(offsets_ref, k, before))
    return off + MOBILITY * (gap_after - gap_before) + row(displace_ref, k, j)


def over_beads(body, start, stop, layers):
    half = layers * LANES
    for low, high, first, size in (
        (0, HEAD_BEADS, 0, half), (HEAD_BEADS, TAIL_BEAD, 0, 2 * half), (TAIL_BEAD, stop, half, half),
    ):
        low, high = max(low, start), min(high, stop)
        if low < high:
            pl.loop(low // GROUP, high // GROUP)(functools.partial(body, first=first, size=size))


def gather_planes(table_ref, hot, first, row):
    size, chains = hot.shape
    width = table_ref.shape[1] // PIECES
    rows = sum(
        jnp.dot(table_ref[:, p * width + first:p * width + first + size], hot, preferred_element_type=F32)
        for p in range(PIECES))
    sub = lax.broadcasted_iota(jnp.int32, (8, chains), 0)
    found = [jnp.zeros((8, chains), F32)] * 2
    for block in range(ROWS // 8):
        mask = sub + 8 * block == row
        for k in range(2):
            at = 8 * (block * 2 + k)
            found[k] = jnp.where(mask, rows[at:at + 8], found[k])
    return [jnp.sum(part, axis=0, keepdims=True) * (1 / FORCE_SCALE) for part in found]


def write_planes(table_ref, at, forces):
    width = table_ref.shape[1] // PIECES
    rows = jnp.concatenate(
        [force[8 * block:8 * block + 8] for block in range(ROWS // 8) for force in forces], axis=0)
    for p, piece in enumerate(split_e4(rows * FORCE_SCALE)):
        table_ref[:, p * width + at:p * width + at + LANES] = piece


def gather_rise(table_ref, hot, first, row):
    size, chains = hot.shape
    rows = jnp.dot(table_ref[:, first:first + size], hot, preferred_element_type=F32)
    sub = lax.broadcasted_iota(jnp.int32, (8, chains), 0)
    found = [jnp.zeros((8, chains), F32)] * PIECES
    for block in range(ROWS // 8):
        mask = sub + 8 * block == row
        for p in range(PIECES):
            at = 8 * (block * PIECES + p)
            found[p] = jnp.where(mask, rows[at:at + 8], found[p])
    return jnp.sum(sum(found), axis=0, keepdims=True) * (1 / FORCE_SCALE)


def write_rise(table_ref, at, force):
    pieces = [piece.astype(F32) for piece in split_e4(force * FORCE_SCALE)]
    rows = [piece[8 * block:8 * block + 8] for block in range(ROWS // 8) for piece in pieces]
    table_ref[:, at:at + LANES] = jnp.concatenate(rows, axis=0).astype(E4)


def plane_beads(start, stop, layers, chains, cells_ref, split_ref, base_ref, table_ref, new_ref):
    width = 2 * layers * LANES

    def body(g, first, size):
        for slot in range(GROUP):
            j = g * GROUP + slot
            row, column = bead_keys(cells_ref, split_ref, j, chains, layers, size == width)
            for k, push in enumerate(gather_planes(table_ref, one_hot_e4(size, column), first, row)):
                new_ref[k:k + 1, pl.ds(pl.multiple_of(j * chains, chains), chains)] = (
                    bead_row(base_ref, k, j, chains) + MOBILITY * push)

    over_beads(body, start, stop, layers)


def slot_lanes(beads, slots):
    lane = lax.broadcasted_iota(jnp.int32, (1, beads * slots), 1)
    return lane // slots, lane % slots


def picker(chosen_ref, way, beads, chains):
    slots = chosen_ref.shape[2]
    chosen = jnp.concatenate([chosen_ref[0, way:way + 1, :]] * beads, axis=1)
    hot = lax.broadcasted_iota(jnp.int32, (chains, beads * slots), 0) == chosen
    hot = jnp.where(hot, 1.0, 0.0).astype(BF16)
    bead_of, _ = slot_lanes(beads, slots)
    own = lax.broadcasted_iota(jnp.int32, (beads, beads * slots), 0) == bead_of

    def pick(pieces):
        got = jnp.dot(jnp.concatenate(pieces, axis=0), hot, preferred_element_type=F32)
        return [
            jnp.sum(jnp.where(own, got[p * beads:(p + 1) * beads], 0.0), axis=0, keepdims=True)
            for p in range(len(pieces))
        ]

    return pick


def early_kernel(layers, beads, chains, cells_ref, offsets_ref, displace_ref, split_ref, field_ref,
                 chosen_ref, used_ref, base_ref, table_ref, picked_ref, place_ref):
    width = 2 * layers * LANES
    for species in range(2):
        for layer in range(layers):
            plane = field_ref[species, layer]
            at = (species * layers + layer) * LANES
            write_planes(table_ref, at, [force_x(plane), force_y(plane)])

    @pl.loop(0, beads)
    def _(j):
        for k in range(3):
            place_ref[k, pl.ds(j, 1), :] = bead_row(cells_ref, k, j, chains).astype(F32)
        for k in range(2):
            row = base_row(cells_ref, offsets_ref, displace_ref, k, j, chains, beads)
            base_ref[k:k + 1, pl.ds(pl.multiple_of(j * chains, chains), chains)] = row
            place_ref[3 + k, pl.ds(j, 1), :] = row

    cells = [place_ref[k].astype(BF16) for k in range(3)]
    bases = [piece for k in range(2) for piece in split_three(place_ref[3 + k])]
    split = jnp.broadcast_to(split_ref[...], (beads, chains)).astype(F32).astype(BF16)
    bead_of, slot_of = slot_lanes(beads, chosen_ref.shape[2])
    for way in range(2):
        x, y, z, edge, *pieces = picker(chosen_ref, way, beads, chains)([*cells, split, *bases])
        row, column = key_row(*(value.astype(jnp.int32) for value in (x, y, z)))
        column = column + jnp.where(bead_of >= edge.astype(jnp.int32), layers * LANES, 0)
        pushes = gather_planes(table_ref, one_hot_e4(width, column), 0, row)
        kept = slot_of < used_ref[0, way]
        for k, (cell, push) in enumerate(zip((x, y), pushes)):
            base = sum(pieces[3 * k:3 * k + 3])
            picked_ref[way, k:k + 1, :] = jnp.where(kept, cell + (base + MOBILITY * push), 0.0)


def first_kernel(start, stop, layers, chains, *refs):
    plane_beads(start, stop, layers, chains, *refs)


def rest_kernel(start, stop, layers, chains, cells_ref, split_ref, base_ref, table_ref, flat_ref, rise_ref, new_ref):
    new_ref[0:2, 0:start * chains] = flat_ref[...]
    new_ref[2:3, :] = rise_ref[...]
    plane_beads(start, stop, layers, chains, cells_ref, split_ref, base_ref, table_ref, new_ref)


def rise_kernel(layers, beads, chains, cells_ref, offsets_ref, displace_ref, split_ref, field_ref,
                below_ref, above_ref, chosen_ref, used_ref, picked_ref, rise_ref, sums_ref, carry_ref, fall_ref,
                table_ref, hot_ref, weight_ref, total_ref, place_ref):
    width = 2 * layers * LANES
    for species in range(2):
        stack = [below_ref[species]] + [field_ref[species, k] for k in range(layers)] + [above_ref[species]]
        for layer in range(layers):
            at = (species * layers + layer) * LANES
            write_rise(table_ref, at, (stack[layer] - stack[layer + 2]) * 0.5)
    total_ref[...] = jnp.zeros_like(total_ref)

    def body(g, first, size):
        for slot in range(GROUP):
            j = g * GROUP + slot
            lanes = slice(slot * chains, (slot + 1) * chains)
            row, column = bead_keys(cells_ref, split_ref, j, chains, layers, size == width)
            hot = one_hot_e4(size, column)
            hot_ref[0:size, lanes] = hot
            push = gather_rise(table_ref, hot, first, row)
            new = base_row(cells_ref, offsets_ref, displace_ref, 2, j, chains, beads) + MOBILITY * push
            place_ref[pl.ds(j, 1), :] = bead_row(cells_ref, 2, j, chains).astype(F32) + new
            rise_ref[0:1, pl.ds(pl.multiple_of(j * chains, chains), chains)] = new
            pieces = [jnp.ones(new.shape, E4)] + split_e4(jnp.clip(new, 0.0, 1.0) * SHARE_SCALE)
            for b, block in enumerate(masks_e4(ROWS, row)):
                step = block.shape[0]
                for p, piece in enumerate(pieces):
                    weight_ref[p * ROWS + b * step:p * ROWS + (b + 1) * step, lanes] = jnp.where(
                        block, jnp.broadcast_to(piece, block.shape), jnp.zeros((), E4))
        total_ref[:, first:first + size] += lax.dot_general(
            weight_ref[...], hot_ref[0:size, :], (((1,), (1,)), ((), ())), preferred_element_type=F32)

    over_beads(body, 0, beads, layers)

    blocks = sums_ref.shape[0]
    per = ROWS // (2 * blocks)
    places = [rep_place(2 * blocks, rep) for rep in range(2 * blocks)]
    for species in range(2):
        upper = None
        for layer in range(layers):
            at = (species * layers + layer) * LANES
            count, *rises = (total_ref[p * ROWS:(p + 1) * ROWS, at:at + LANES] for p in range(1 + PIECES))
            rise = sum(rises) * (1 / SHARE_SCALE)
            lower = count - rise if upper is None else count - rise + upper
            for rep, (block, half) in enumerate(places):
                slab = (half * 2 * layers + layer * 2 + species) * per
                sums_ref[block, slab:slab + per, :] = lower[rep * per:(rep + 1) * per]
            upper = rise
        for rep, (block, half) in enumerate(places):
            slab = (half * 2 + species) * per
            carry_ref[block, slab:slab + per, :] = upper[rep * per:(rep + 1) * per]

    def lay(ref, line):
        for k in range(3):
            for n in range(chains // LANES):
                at = k * (chains // LANES) + n
                ref[at:at + 1, :] = line[k][:, n * LANES:(n + 1) * LANES]

    slots = chosen_ref.shape[2]
    carry_ref[blocks] = jnp.zeros(carry_ref.shape[1:], F32)
    pieces = split_three(place_ref[...])
    _, slot_of = slot_lanes(beads, slots)
    for way, (ref, lift) in enumerate(((carry_ref.at[blocks], -float(layers)), (fall_ref, float(layers)))):
        line = sum(picker(chosen_ref, way, beads, chains)(pieces)) + lift
        line = jnp.where(slot_of < used_ref[0, way], line, 0.0)
        lay(ref, [picked_ref[way, 0:1, :], picked_ref[way, 1:2, :], line])


def merge_kernel(sums_ref, carried_ref, merged_ref):
    blocks, rows, _ = sums_ref.shape
    merged_ref[...] = sums_ref[...]
    for half in range(2):
        at, carry = slice(half * rows // 2, half * rows // 2 + rows // 4), slice(half * rows // 4, (half + 1) * rows // 4)
        merged_ref[:, at, :] = sums_ref[:, at, :] + carried_ref[0:blocks, carry, :]


def fold_kernel(parts_ref, carried_ref, fallen_ref, folded_ref):
    blocks, rows, _ = parts_ref.shape
    extra = fallen_ref.shape[0]
    total = jnp.sum(parts_ref[...], axis=0)
    for half in range(2):
        folded_ref[half, 0:rows // 2, :] = total[half * rows // 2:(half + 1) * rows // 2]
        folded_ref[half, rows // 2:rows // 2 + extra, :] = carried_ref[blocks, 0:extra, :]
        folded_ref[half, rows // 2 + extra:, :] = fallen_ref[...]


def last_kernel(layers, scale, both_ref, carried_ref, fallen_ref, own_ref, density_ref, arrived_ref):
    blocks = carried_ref.shape[0] - 1
    per = density_ref.shape[2] // LANES
    rows, extra = 2 * layers * per, fallen_ref.shape[0]
    total = (both_ref[0, 0:rows, :] + both_ref[1, 0:rows, :]) * scale
    for layer in range(layers):
        for species in range(2):
            for n in range(per):
                at = (layer * 2 + species) * per + n
                density_ref[species, layer:layer + 1, n * LANES:(n + 1) * LANES] = total[at:at + 1]
    other = jnp.where(own_ref[0] == 0, both_ref[1, rows:, :], both_ref[0, rows:, :])
    up = jnp.where(own_ref[1] == 1, other[0:extra], carried_ref[blocks, 0:extra, :])
    down = jnp.where(own_ref[2] == 1, other[extra:], fallen_ref[...])
    for way, came in enumerate((up, down)):
        for k in range(3):
            for n in range(extra // 3):
                at = k * (extra // 3) + n
                arrived_ref[k, way:way + 1, n * LANES:(n + 1) * LANES] = came[at:at + 1]


def local_call(kernel, name, shapes, scratch, operands, scalars=(), limit=24):
    return pl.pallas_call(
        kernel,
        out_shape=tuple(jax.ShapeDtypeStruct(shape, dtype) for shape, dtype in shapes),
        in_specs=[
            pl.BlockSpec(memory_space=pltpu.SMEM if n in scalars else pltpu.VMEM) for n in range(len(operands))],
        out_specs=tuple([pl.BlockSpec(memory_space=pltpu.VMEM)] * len(shapes)),
        scratch_shapes=[pltpu.VMEM(shape, dtype) for shape, dtype in scratch],
        compiler_params=pltpu.CompilerParams(vmem_limit_bytes=limit * 1024 * 1024),
        name=name,
    )(*operands)


def rep_place(reps, rep):
    turn = reps // 8
    return rep // (2 * turn) * turn + rep % turn, rep // turn % 2


def rep_groups(reps):
    halves = [[rep for rep in range(reps) if rep_place(reps, rep)[1] == half] for half in range(2)]
    return halves, [list(pair) for pair in zip(*halves)]


def exchange(value, groups):
    return lax.all_to_all(value, "rep", split_axis=0, concat_axis=0, tiled=True, axis_index_groups=groups)


def ring(value, steps):
    doms, reps = lax.axis_size("dom"), lax.axis_size("rep")
    pairs = []
    for dom in range(doms):
        for rep in range(reps):
            turn = 0 if 0 <= dom + steps < doms else reps // 8
            pairs.append((dom * reps + rep, (dom + steps) % doms * reps + (rep ^ turn)))
    return lax.ppermute(value, ("dom", "rep"), pairs)


def shards(cells, offsets, displacements, block_split, fields, crossing, crossing_counts):
    chains = block_split.shape[0]
    beads = cells.shape[1] // chains
    layers = fields.shape[1]
    doms, reps = lax.axis_size("dom"), lax.axis_size("rep")
    dom, rep = lax.axis_index("dom"), lax.axis_index("rep")
    blocks, extra = reps // 2, 3 * chains // LANES
    rows = 4 * layers * (ROWS // reps)
    halves, pairs = rep_groups(reps)
    width = 2 * layers * LANES
    sizes = (layers, beads, chains)
    planes = fields.reshape(2, layers, ROWS, LANES)
    split = block_split[None]
    beads_in = (cells, offsets, displacements, split)
    own = jnp.stack([rep_place(reps, rep)[1], dom == 0, dom == doms - 1]).astype(jnp.int32)

    below = ring(planes[:, -1], 1)
    above = ring(planes[:, 0], -1)
    base, table, picked = local_call(
        functools.partial(early_kernel, *sizes), "early_step",
        (((2, beads * chains), F32), ((2 * ROWS, PIECES * width), E4), ((2, 2, chains), F32)),
        (((5, beads, chains), F32),), (*beads_in, planes, crossing, crossing_counts), (6,))
    below, above, picked = lax.optimization_barrier((below, above, picked))
    rise, sums, carry, fall = local_call(
        functools.partial(rise_kernel, *sizes), "rise_step",
        (((1, beads * chains), F32), ((blocks, rows, LANES), F32),
         ((blocks + 1, rows // 2, LANES), F32), ((extra, LANES), F32)),
        (((PIECES * ROWS, width), E4), ((width, GROUP * chains), E4),
         (((1 + PIECES) * ROWS, GROUP * chains), E4), (((1 + PIECES) * ROWS, width), F32), ((beads, chains), F32)),
        (*beads_in, planes, below, above, crossing, crossing_counts, picked), (8,))
    carried, fallen = ring(carry, 1), ring(fall, -1)
    merged, = local_call(
        merge_kernel, "merge_step", (((blocks, rows, LANES), F32),), (), (sums, carried), limit=8)

    merged, base = lax.optimization_barrier((merged, base))
    parts = exchange(merged, halves)
    flat, = local_call(
        functools.partial(first_kernel, 0, FIRST_BEADS, layers, chains), "first_step",
        (((2, FIRST_BEADS * chains), F32),), (), (cells, split, base, table))
    parts, flat = lax.optimization_barrier((parts, flat))
    folded, = local_call(
        fold_kernel, "fold_step", (((2, rows // 2 + 2 * extra, LANES), F32),), (), (parts, carried, fallen), limit=8)
    folded, base = lax.optimization_barrier((folded, base))
    both = exchange(folded, pairs)
    new, = local_call(
        functools.partial(rest_kernel, FIRST_BEADS, beads, layers, chains), "rest_step",
        (((3, beads * chains), F32),), (), (cells, split, base, table, flat, rise))
    both, new = lax.optimization_barrier((both, new))
    density_scale = GRID * GRID * layers / (reps * chains * beads)
    density, arrived = local_call(
        functools.partial(last_kernel, layers, density_scale), "last_step",
        (((2, layers, CELLS // reps), F32), ((3, 2, chains), F32)), (), (both, carried, fallen, own), (3,), limit=8)
    return new, density, arrived.transpose(1, 0, 2)


def solution(mesh):
    in_specs = (
        P(None, ("dom", "rep")),
        P(None, ("dom", "rep")),
        P(None, ("dom", "rep")),
        P(("dom", "rep")),
        P(None, "dom", None),
        P(("dom", "rep"), None, None),
        P(("dom", "rep"), None),
    )
    out_specs = (P(None, ("dom", "rep")), P(None, "dom", "rep"), P(None, None, ("dom", "rep")))
    return jax.shard_map(shards, mesh=mesh, in_specs=in_specs, out_specs=out_specs, check_vma=False)
```

time: 99 us -> 82.3 us (0.83)
  the two profiles are of different devices: /device:TPU:32 before, /device:TPU:1 now
where the time goes in v3:
time: 82.3 us; the launch traced here: 81 us
  Pallas kernels  37.1 us (45%)
  starting transfers between devices  29.6 us (36%)
  waiting for transfers between devices  11.8 us (14%)
  local copies, waits for them, and re-layouts  1.64 us (2%)
    pallas_call x7, Pallas kernels, local_call(): pl.pallas_call(kernel, out_shape=tuple((jax.ShapeDtypeStruct(shape, dtype...  37.1 us
    all_to_all x2, starting transfers between devices, exchange(): lax.all_to_all(value, 'rep', split_axis=0, concat_axis=0, tiled=True, axi...  15.5 us
    ppermute x4, starting transfers between devices, ring(): return lax.ppermute(value, ('dom', 'rep'), pairs)  14.1 us
    all_to_all x2, waiting for transfers between devices, exchange(): lax.all_to_all(value, 'rep', split_axis=0, concat_axis=0, tiled=True, axi...  6.9 us
    ppermute x4, waiting for transfers between devices, ring(): return lax.ppermute(value, ('dom', 'rep'), pairs)  4.89 us
  transfers between devices with their start and end apart: 6, of which 2 were waited for; matrix products, arithmetic and copies ran while one was open for 0% of the time, Pallas kernels for 21%

profile of v3, /device:TPU:1, one launch (start us, length us, event | category | flops | bytes accessed | tf_op | source)
XLA Modules:
  0.0 81.0 jit_solution(438576499017680129)
XLA Ops:
  0.6 1.6 %reshape.12.field_ref = f32[2,2,288,128]{3,2,1,0:T(8,128)S(1)} reshape(f32[2,2,36864]{2,1,0:T(2,128)} %param.11) | data formatting | bytes 1179648 | tf_op jit(solution)/shard_map/reshape | solution.py:406
  2.2 0.0 copy-start
  2.2 0.0 copy-start.1
  2.2 0.0 copy-start.2
  2.3 0.0 copy-start.3
  2.3 3.0 %collective-permute-start = (f32[2,288,128]{2,1,0:T(8,128)S(1)}, f32[2,288,128]{2,1,0:T(8,128)S(1)}, u32[]{:S(2)}, u32[]{:S(2)}) collective-permute-start(f32[2,288,128]{2,1,0:T(8,128)S(1)} %get-tuple-element.44), channel_id=1, source_target_pairs={{0,32},{1,33},{2,34},{3,35},{4,36},{5,37},{6,38},{7,39},{8,40},{9,... | collective-permute-start | bytes 884744 | tf_op jit(solution)/shard_map/ppermute | solution.py:392
  5.3 0.0 copy-start.4
  5.3 0.0 copy-start.5
  5.3 3.9 %collective-permute-start.1 = (f32[2,288,128]{2,1,0:T(8,128)S(1)}, f32[2,288,128]{2,1,0:T(8,128)S(1)}, u32[]{:S(2)}, u32[]{:S(2)}) collective-permute-start(f32[2,288,128]{2,1,0:T(8,128)S(1)} %get-tuple-element.43), channel_id=1, source_target_pairs={{0,484},{1,485},{2,486},{3,487},{4,480},{5,481},{6,482},{7,483},{8... | collective-permute-start | bytes 884744 | tf_op jit(solution)/shard_map/ppermute | solution.py:392
  9.2 0.0 copy-done
  9.2 0.0 copy-done.1
  9.2 0.0 copy-done.2
  9.3 0.0 copy-done.3
  9.3 0.0 copy-done.4
  9.3 0.0 copy-done.5
  9.3 4.1 %early_step.1 = (f32[2,16384]{1,0:T(2,128)S(1)}, f8e4m3fn[576,1536]{1,0:T(32,128)(4,1)S(1)}, f32[2,2,512]{2,1,0:T(2,128)S(1)}) custom-call(s32[3,16384]{1,0:T(4,128)S(1)} %copy-done, f32[3,16384]{1,0:T(4,128)S(1)} %copy-done.1, f32[3,16384]{1,0:T(4,128)S(1)} %copy-done.2, s32[1,512]{1,0:T(1,128)S(1)} %bitcast.13, f32[2,2,288,128]{3,2,1,0:T(8,128)S(1)} %reshape.12.field_ref, ...), custom_call_target="tpu_custom_call" | custom-call | tf_op jit(solution)/shard_map/early_step/pallas_call | solution.py:359
  13.4 0.0 collective-permute-done.below_ref
  13.4 0.0 collective-permute-done.1.above_ref
  13.4 17.2 %rise_step.1 = (f32[1,16384]{1,0:T(1,128)S(1)}, f32[16,72,128]{2,1,0:T(8,128)S(1)}, f32[17,36,128]{2,1,0:T(8,128)S(1)}, f32[12,128]{1,0:T(8,128)S(1)}) custom-call(s32[3,16384]{1,0:T(4,128)S(1)} %copy-done, f32[3,16384]{1,0:T(4,128)S(1)} %copy-done.1, f32[3,16384]{1,0:T(4,128)S(1)} %copy-done.2, s32[1,512]{1,0:T(1,128)S(1)} %bitcast.14, ...), custom_call_target="tpu_custom_call" | custom-call | tf_op jit(solution)/shard_map/rise_step/pallas_call | solution.py:359
  30.7 0.0 collective-permute-start.2
  30.7 4.9 %collective-permute-done.2.carried_ref = f32[17,36,128]{2,1,0:T(8,128)S(1)} collective-permute-done((f32[17,36,128]{2,1,0:T(8,128)S(1)}, f32[17,36,128]{2,1,0:T(8,128)S(1)}, u32[]{:S(2)}, u32[]{:S(2)}) %collective-permute-start.2) | collective-permute-done | bytes 313376 | tf_op jit(solution)/shard_map/ppermute | solution.py:392
  35.6 0.9 %merge_step.1 = f32[16,72,128]{2,1,0:T(8,128)} custom-call(f32[16,72,128]{2,1,0:T(8,128)S(1)} %get-tuple-element.27.sums_ref, f32[17,36,128]{2,1,0:T(8,128)S(1)} %collective-permute-done.2.carried_ref), custom_call_target="tpu_custom_call" | custom-call | tf_op jit(solution)/shard_map/merge_step/pallas_call | solution.py:359
  36.5 6.8 %all-to-all-start = ((f32[16,72,128]{2,1,0:T(8,128)}), f32[16,72,128]{2,1,0:T(8,128)S(1)}, u32[]{:S(2)}, u32[]{:S(2)}) async-start(f32[16,72,128]{2,1,0:T(8,128)} %merge_step.1), calls=%async_computation | async-start | bytes 1179648 | tf_op jit(solution)/shard_map/all_to_all | solution.py:382
  43.2 7.1 %collective-permute-start.3 = (f32[12,128]{1,0:T(8,128)S(1)}, f32[12,128]{1,0:T(8,128)S(1)}, u32[]{:S(2)}, u32[]{:S(2)}) collective-permute-start(f32[12,128]{1,0:T(8,128)S(1)} %get-tuple-element.34), channel_id=1, source_target_pairs={{0,484},{1,485},{2,486},{3,487},{4,480},{5,481},{6,482},{7,483},{8... | collective-permute-start | bytes 18440 | tf_op jit(solution)/shard_map/ppermute | solution.py:392
  50.4 8.1 %first_step.1.flat_ref = f32[2,10240]{1,0:T(2,128)S(1)} custom-call(s32[3,16384]{1,0:T(4,128)S(1)} %copy-done, s32[1,512]{1,0:T(1,128)S(1)} %bitcast.15, f32[2,16384]{1,0:T(2,128)S(1)} %get-tuple-element.36.refs_2_.base_ref, f8e4m3fn[576,1536]{1,0:T(32,128)(4,1)S(1)} %get-tuple-element.32.refs_3_.table_ref), custom_call_target="tpu_custom_call" | custom-call | tf_op jit(solution)/shard_map/first_step/pallas_call | solution.py:359
  58.5 0.0 all-to-all-done.parts_ref
  58.5 0.0 collective-permute-done.3.fallen_ref
  58.5 0.7 fold_step.1
  59.2 8.8 %all-to-all-start.1 = ((f32[2,60,128]{2,1,0:T(8,128)}), f32[2,60,128]{2,1,0:T(8,128)S(1)}, u32[]{:S(2)}, u32[]{:S(2)}) async-start(f32[2,60,128]{2,1,0:T(8,128)} %fold_step.1), calls=%async_computation.1 | async-start | bytes 131072 | tf_op jit(solution)/shard_map/all_to_all | solution.py:382
  68.0 0.1 pad_add_fusion.own_ref
  68.0 4.9 %rest_step.1 = f32[3,16384]{1,0:T(4,128)} custom-call(s32[3,16384]{1,0:T(4,128)S(1)} %copy-done, s32[1,512]{1,0:T(1,128)S(1)} %bitcast.16, f32[2,16384]{1,0:T(2,128)S(1)} %get-tuple-element.36.refs_2_.base_ref, f8e4m3fn[576,1536]{1,0:T(32,128)(4,1)S(1)} %get-tuple-element.32.refs_3_.table_ref, f32[2,10240]{1,0:T(2,128)S(1)} %first_step.1.flat_ref, ...), custom_call_target="tpu_custom_call" | custom-call | tf_op jit(solution)/shard_map/rest_step/pallas_call | solution.py:359
  72.9 6.9 %all-to-all-done.1.both_ref = f32[2,60,128]{2,1,0:T(8,128)S(1)} async-done(((f32[2,60,128]{2,1,0:T(8,128)}), f32[2,60,128]{2,1,0:T(8,128)S(1)}, u32[]{:S(2)}, u32[]{:S(2)}) %all-to-all-start.1) | async-done | bytes 61472 | tf_op jit(solution)/shard_map/all_to_all | solution.py:382
  79.8 1.2 %last_step.1 = (f32[2,2,1152]{2,1,0:T(2,128)}, f32[3,2,512]{2,1,0:T(2,128)}) custom-call(f32[2,60,128]{2,1,0:T(8,128)S(1)} %all-to-all-done.1.both_ref, f32[17,36,128]{2,1,0:T(8,128)S(1)} %collective-permute-done.2.carried_ref, f32[12,128]{1,0:T(8,128)S(1)} %collective-permute-done.3.fallen_ref, s32[3]{0:T(128)S(1)} %pad_add_fusion.own_ref), custom_call_target="tpu_custom_call" | custom-call | tf_op jit(solution)/shard_map/last_step/pallas_call | solution.py:359
  (1 shorter events, 0.0 us)
Async XLA Ops:
  2.2 7.0 %copy-start = (s32[3,16384]{1,0:T(4,128)S(1)}, s32[3,16384]{1,0:T(4,128)}, u32[]{:S(2)}) copy-start(s32[3,16384]{1,0:T(4,128)} %cells_ref.5) | copy-start | bytes 589828
  2.2 7.0 %copy-start.1 = (f32[3,16384]{1,0:T(4,128)S(1)}, f32[3,16384]{1,0:T(4,128)}, u32[]{:S(2)}) copy-start(f32[3,16384]{1,0:T(4,128)} %offsets_ref.3) | copy-start | bytes 589828
  2.2 7.0 %copy-start.2 = (f32[3,16384]{1,0:T(4,128)S(1)}, f32[3,16384]{1,0:T(4,128)}, u32[]{:S(2)}) copy-start(f32[3,16384]{1,0:T(4,128)} %displace_ref.3) | copy-start | bytes 589828
  2.3 7.0 %copy-start.3 = (s32[512]{0:T(512)S(1)}, s32[512]{0:T(512)}, u32[]{:S(2)}) copy-start(s32[512]{0:T(512)} %param.10) | copy-start | bytes 6148
  2.3 11.1 %collective-permute-start = (f32[2,288,128]{2,1,0:T(8,128)S(1)}, f32[2,288,128]{2,1,0:T(8,128)S(1)}, u32[]{:S(2)}, u32[]{:S(2)}) collective-permute-start(f32[2,288,128]{2,1,0:T(8,128)S(1)} %get-tuple-element.44), channel_id=1, source_target_pairs={{0,32},{1,33},{2,34},{3,35},{4,36},{5,37},{6,38},{7,39},{8,40},{9,... | collective-permute-start | bytes 884744 | tf_op jit(solution)/shard_map/ppermute | solution.py:392
  5.3 3.9 %copy-start.4 = (s32[1,2,16]{2,1,0:T(2,128)S(1)}, s32[1,2,16]{2,1,0:T(2,128)}, u32[]{:S(2)}) copy-start(s32[1,2,16]{2,1,0:T(2,128)} %chosen_ref.3) | copy-start | bytes 388
  5.3 3.9 %copy-start.5 = (s32[1,2]{1,0:T(1,128)S(1)}, s32[1,2]{1,0:T(1,128)}, u32[]{:S(2)}) copy-start(s32[1,2]{1,0:T(1,128)} %used_ref.3) | copy-start | bytes 28
  5.3 8.1 %collective-permute-start.1 = (f32[2,288,128]{2,1,0:T(8,128)S(1)}, f32[2,288,128]{2,1,0:T(8,128)S(1)}, u32[]{:S(2)}, u32[]{:S(2)}) collective-permute-start(f32[2,288,128]{2,1,0:T(8,128)S(1)} %get-tuple-element.43), channel_id=1, source_target_pairs={{0,484},{1,485},{2,486},{3,487},{4,480},{5,481},{6,482},{7,483},{8... | collective-permute-start | bytes 884744 | tf_op jit(solution)/shard_map/ppermute | solution.py:392
  30.7 4.9 %collective-permute-start.2 = (f32[17,36,128]{2,1,0:T(8,128)S(1)}, f32[17,36,128]{2,1,0:T(8,128)S(1)}, u32[]{:S(2)}, u32[]{:S(2)}) collective-permute-start(f32[17,36,128]{2,1,0:T(8,128)S(1)} %get-tuple-element.28), channel_id=1, source_target_pairs={{0,32},{1,33},{2,34},{3,35},{4,36},{5,37},{6,38},{7,39},{8,40},{9,... | collective-permute-start | bytes 940040 | tf_op jit(solution)/shard_map/ppermute | solution.py:392
  36.5 22.0 %all-to-all-start = ((f32[16,72,128]{2,1,0:T(8,128)}), f32[16,72,128]{2,1,0:T(8,128)S(1)}, u32[]{:S(2)}, u32[]{:S(2)}) async-start(f32[16,72,128]{2,1,0:T(8,128)} %merge_step.1), calls=%async_computation | async-start | bytes 1179648 | tf_op jit(solution)/shard_map/all_to_all | solution.py:382
  43.2 15.2 %collective-permute-start.3 = (f32[12,128]{1,0:T(8,128)S(1)}, f32[12,128]{1,0:T(8,128)S(1)}, u32[]{:S(2)}, u32[]{:S(2)}) collective-permute-start(f32[12,128]{1,0:T(8,128)S(1)} %get-tuple-element.34), channel_id=1, source_target_pairs={{0,484},{1,485},{2,486},{3,487},{4,480},{5,481},{6,482},{7,483},{8... | collective-permute-start | bytes 18440 | tf_op jit(solution)/shard_map/ppermute | solution.py:392
  59.2 20.6 %all-to-all-start.1 = ((f32[2,60,128]{2,1,0:T(8,128)}), f32[2,60,128]{2,1,0:T(8,128)S(1)}, u32[]{:S(2)}, u32[]{:S(2)}) async-start(f32[2,60,128]{2,1,0:T(8,128)} %fold_step.1), calls=%async_computation.1 | async-start | bytes 131072 | tf_op jit(solution)/shard_map/all_to_all | solution.py:382

commit v4 on v3

--- a/solution.py
+++ b/solution.py
@@ -14,8 +14,9 @@
 MOBILITY = 0.1
 HEAD_BEADS = 8
 TAIL_BEAD = 24
-GROUP = 4
-FIRST_BEADS = 20
+GROUP = 8
+HALF_GROUP = 4
+FIRST_BEADS = 16
 F32 = jnp.float32
 BF16 = jnp.bfloat16
 
@@ -252,7 +253,7 @@
 
 def rise_kernel(layers, beads, chains, cells_ref, offsets_ref, displace_ref, split_ref, field_ref,
                 below_ref, above_ref, chosen_ref, used_ref, picked_ref, rise_ref, sums_ref, carry_ref, fall_ref,
-                table_ref, hot_ref, weight_ref, total_ref, place_ref):
+                table_ref, hot_refs, weight_refs, total_ref, place_ref):
     width = 2 * layers * LANES
     for species in range(2):
         stack = [below_ref[species]] + [field_ref[species, k] for k in range(layers)] + [above_ref[species]]
@@ -261,25 +262,34 @@
             write_rise(table_ref, at, (stack[layer] - stack[layer + 2]) * 0.5)
     total_ref[...] = jnp.zeros_like(total_ref)
 
+    def move(j, slot, first, size, hot_ref, weight_ref):
+        lanes = slice(slot * chains, (slot + 1) * chains)
+        row, column = bead_keys(cells_ref, split_ref, j, chains, layers, size == width)
+        hot = one_hot_e4(size, column)
+        hot_ref[0:size, lanes] = hot
+        push = gather_rise(table_ref, hot, first, row)
+        new = base_row(cells_ref, offsets_ref, displace_ref, 2, j, chains, beads) + MOBILITY * push
+        place_ref[pl.ds(j, 1), :] = bead_row(cells_ref, 2, j, chains).astype(F32) + new
+        rise_ref[0:1, pl.ds(pl.multiple_of(j * chains, chains), chains)] = new
+        pieces = [jnp.ones(new.shape, E4)] + split_e4(jnp.clip(new, 0.0, 1.0) * SHARE_SCALE)
+        for b, block in enumerate(masks_e4(ROWS, row)):
+            step = block.shape[0]
+            for p, piece in enumerate(pieces):
+                weight_ref[p * ROWS + b * step:p * ROWS + (b + 1) * step, lanes] = jnp.where(
+                    block, jnp.broadcast_to(piece, block.shape), jnp.zeros((), E4))
+
     def body(g, first, size):
-        for slot in range(GROUP):
-            j = g * GROUP + slot
-            lanes = slice(slot * chains, (slot + 1) * chains)
-            row, column = bead_keys(cells_ref, split_ref, j, chains, layers, size == width)
-            hot = one_hot_e4(size, column)
-            hot_ref[0:size, lanes] = hot
-            push = gather_rise(table_ref, hot, first, row)
-            new = base_row(cells_ref, offsets_ref, displace_ref, 2, j, chains, beads) + MOBILITY * push
-            place_ref[pl.ds(j, 1), :] = bead_row(cells_ref, 2, j, chains).astype(F32) + new
-            rise_ref[0:1, pl.ds(pl.multiple_of(j * chains, chains), chains)] = new
-            pieces = [jnp.ones(new.shape, E4)] + split_e4(jnp.clip(new, 0.0, 1.0) * SHARE_SCALE)
-            for b, block in enumerate(masks_e4(ROWS, row)):
-                step = block.shape[0]
-                for p, piece in enumerate(pieces):
-                    weight_ref[p * ROWS + b * step:p * ROWS + (b + 1) * step, lanes] = jnp.where(
-                        block, jnp.broadcast_to(piece, block.shape), jnp.zeros((), E4))
-        total_ref[:, first:first + size] += lax.dot_general(
-            weight_ref[...], hot_ref[0:size, :], (((1,), (1,)), ((), ())), preferred_element_type=F32)
+        def add_up(half, low, high):
+            total_ref[low:high, first:first + size] += lax.dot_general(
+                weight_refs[half][low:high, :], hot_refs[half][0:size, :], (((1,), (1,)), ((), ())),
+                preferred_element_type=F32)
+
+        for slot in range(HALF_GROUP):
+            move(g * GROUP + slot, slot, first, size, hot_refs[0], weight_refs[0])
+        for slot in range(HALF_GROUP):
+            move(g * GROUP + HALF_GROUP + slot, slot, first, size, hot_refs[1], weight_refs[1])
+            add_up(0, slot * ROWS, (slot + 1) * ROWS)
+        add_up(1, 0, weight_refs[1].shape[0])
 
     over_beads(body, 0, beads, layers)
 
@@ -362,7 +372,9 @@
         in_specs=[
             pl.BlockSpec(memory_space=pltpu.SMEM if n in scalars else pltpu.VMEM) for n in range(len(operands))],
         out_specs=tuple([pl.BlockSpec(memory_space=pltpu.VMEM)] * len(shapes)),
-        scratch_shapes=[pltpu.VMEM(shape, dtype) for shape, dtype in scratch],
+        scratch_shapes=[
+            [pltpu.VMEM(*one) for one in entry] if isinstance(entry, list) else pltpu.VMEM(*entry)
+            for entry in scratch],
         compiler_params=pltpu.CompilerParams(vmem_limit_bytes=limit * 1024 * 1024),
         name=name,
     )(*operands)
@@ -419,8 +431,9 @@
         functools.partial(rise_kernel, *sizes), "rise_step",
         (((1, beads * chains), F32), ((blocks, rows, LANES), F32),
          ((blocks + 1, rows // 2, LANES), F32), ((extra, LANES), F32)),
-        (((PIECES * ROWS, width), E4), ((width, GROUP * chains), E4),
-         (((1 + PIECES) * ROWS, GROUP * chains), E4), (((1 + PIECES) * ROWS, width), F32), ((beads, chains), F32)),
+        (((PIECES * ROWS, width), E4), [((width, HALF_GROUP * chains), E4)] * 2,
+         [(((1 + PIECES) * ROWS, HALF_GROUP * chains), E4)] * 2, (((1 + PIECES) * ROWS, width), F32),
+         ((beads, chains), F32)),
         (*beads_in, planes, below, above, crossing, crossing_counts, picked), (8,))
     carried, fallen = ring(carry, 1), ring(fall, -1)
     merged, = local_call(

time: 82.3 us -> 81 us (0.984)
  the two profiles are of different devices: /device:TPU:1 before, /device:TPU:8 now
where the time goes in v4:
time: 81 us; the launch traced here: 80.6 us
  Pallas kernels  34.8 us (43%)
  starting transfers between devices  25.4 us (31%)
  waiting for transfers between devices  17.9 us (22%)
  local copies, waits for them, and re-layouts  1.65 us (2%)
    pallas_call x7, Pallas kernels, local_call(): pl.pallas_call(kernel, out_shape=tuple((jax.ShapeDtypeStruct(shape, dtype...  34.8 us
    all_to_all x2, starting transfers between devices, exchange(): lax.all_to_all(value, 'rep', split_axis=0, concat_axis=0, tiled=True, axi...  16.4 us
    all_to_all x2, waiting for transfers between devices, exchange(): lax.all_to_all(value, 'rep', split_axis=0, concat_axis=0, tiled=True, axi...  9.76 us
    ppermute x4, starting transfers between devices, ring(): return lax.ppermute(value, ('dom', 'rep'), pairs)  9 us
    ppermute x4, waiting for transfers between devices, ring(): return lax.ppermute(value, ('dom', 'rep'), pairs)  8.17 us
  transfers between devices with their start and end apart: 6, of which 4 were waited for; matrix products, arithmetic and copies ran while one was open for 0% of the time, Pallas kernels for 20%

profile of v4, /device:TPU:8, one launch (start us, length us, event | category | flops | bytes accessed | tf_op | source)
XLA Modules:
  0.0 80.6 jit_solution(16431107547002366400)
XLA Ops:
  0.6 1.6 %reshape.12.field_ref = f32[2,2,288,128]{3,2,1,0:T(8,128)S(1)} reshape(f32[2,2,36864]{2,1,0:T(2,128)} %param.11) | data formatting | bytes 1179648 | tf_op jit(solution)/shard_map/reshape | solution.py:418
  2.2 0.0 copy-start
  2.2 0.0 copy-start.1
  2.2 0.0 copy-start.2
  2.3 0.0 copy-start.3
  2.3 0.0 collective-permute-start
  2.3 0.0 copy-start.4
  2.3 0.0 copy-start.5
  2.4 8.9 %collective-permute-start.1 = (f32[2,288,128]{2,1,0:T(8,128)S(1)}, f32[2,288,128]{2,1,0:T(8,128)S(1)}, u32[]{:S(2)}, u32[]{:S(2)}) collective-permute-start(f32[2,288,128]{2,1,0:T(8,128)S(1)} %get-tuple-element.43), channel_id=1, source_target_pairs={{0,484},{1,485},{2,486},{3,487},{4,480},{5,481},{6,482},{7,483},{8... | collective-permute-start | bytes 884744 | tf_op jit(solution)/shard_map/ppermute | solution.py:404
  11.3 0.0 copy-done
  11.3 0.0 copy-done.1
  11.3 0.0 copy-done.2
  11.3 0.0 copy-done.3
  11.3 0.0 copy-done.4
  11.3 0.0 copy-done.5
  11.3 4.1 %early_step.1 = (f32[2,16384]{1,0:T(2,128)S(1)}, f8e4m3fn[576,1536]{1,0:T(32,128)(4,1)S(1)}, f32[2,2,512]{2,1,0:T(2,128)S(1)}) custom-call(s32[3,16384]{1,0:T(4,128)S(1)} %copy-done, f32[3,16384]{1,0:T(4,128)S(1)} %copy-done.1, f32[3,16384]{1,0:T(4,128)S(1)} %copy-done.2, s32[1,512]{1,0:T(1,128)S(1)} %bitcast.13, f32[2,2,288,128]{3,2,1,0:T(8,128)S(1)} %reshape.12.field_ref, ...), custom_call_target="tpu_custom_call" | custom-call | tf_op jit(solution)/shard_map/early_step/pallas_call | solution.py:369
  15.5 0.2 collective-permute-done.below_ref
  15.7 0.0 collective-permute-done.1.above_ref
  15.7 15.8 %rise_step.1 = (f32[1,16384]{1,0:T(1,128)S(1)}, f32[16,72,128]{2,1,0:T(8,128)S(1)}, f32[17,36,128]{2,1,0:T(8,128)S(1)}, f32[12,128]{1,0:T(8,128)S(1)}) custom-call(s32[3,16384]{1,0:T(4,128)S(1)} %copy-done, f32[3,16384]{1,0:T(4,128)S(1)} %copy-done.1, f32[3,16384]{1,0:T(4,128)S(1)} %copy-done.2, s32[1,512]{1,0:T(1,128)S(1)} %bitcast.14, ...), custom_call_target="tpu_custom_call" | custom-call | tf_op jit(solution)/shard_map/rise_step/pallas_call | solution.py:369
  31.5 0.0 collective-permute-start.2
  31.5 8.0 %collective-permute-done.2.carried_ref = f32[17,36,128]{2,1,0:T(8,128)S(1)} collective-permute-done((f32[17,36,128]{2,1,0:T(8,128)S(1)}, f32[17,36,128]{2,1,0:T(8,128)S(1)}, u32[]{:S(2)}, u32[]{:S(2)}) %collective-permute-start.2) | collective-permute-done | bytes 313376 | tf_op jit(solution)/shard_map/ppermute | solution.py:404
  39.5 0.9 %merge_step.1 = f32[16,72,128]{2,1,0:T(8,128)} custom-call(f32[16,72,128]{2,1,0:T(8,128)S(1)} %get-tuple-element.27.sums_ref, f32[17,36,128]{2,1,0:T(8,128)S(1)} %collective-permute-done.2.carried_ref), custom_call_target="tpu_custom_call" | custom-call | tf_op jit(solution)/shard_map/merge_step/pallas_call | solution.py:369
  40.4 7.4 %all-to-all-start = ((f32[16,72,128]{2,1,0:T(8,128)}), f32[16,72,128]{2,1,0:T(8,128)S(1)}, u32[]{:S(2)}, u32[]{:S(2)}) async-start(f32[16,72,128]{2,1,0:T(8,128)} %merge_step.1), calls=%async_computation | async-start | bytes 1179648 | tf_op jit(solution)/shard_map/all_to_all | solution.py:394
  47.8 0.0 collective-permute-start.3
  47.8 5.7 %first_step.1.flat_ref = f32[2,8192]{1,0:T(2,128)S(1)} custom-call(s32[3,16384]{1,0:T(4,128)S(1)} %copy-done, s32[1,512]{1,0:T(1,128)S(1)} %bitcast.15, f32[2,16384]{1,0:T(2,128)S(1)} %get-tuple-element.36.refs_2_.base_ref, f8e4m3fn[576,1536]{1,0:T(32,128)(4,1)S(1)} %get-tuple-element.32.refs_3_.table_ref), custom_call_target="tpu_custom_call" | custom-call | tf_op jit(solution)/shard_map/first_step/pallas_call | solution.py:369
  53.5 3.4 %all-to-all-done.parts_ref = f32[16,72,128]{2,1,0:T(8,128)S(1)} async-done(((f32[16,72,128]{2,1,0:T(8,128)}), f32[16,72,128]{2,1,0:T(8,128)S(1)}, u32[]{:S(2)}, u32[]{:S(2)}) %all-to-all-start) | async-done | bytes 589856 | tf_op jit(solution)/shard_map/all_to_all | solution.py:394
  56.9 0.0 collective-permute-done.3.fallen_ref
  56.9 0.7 fold_step.1
  57.6 9.1 %all-to-all-start.1 = ((f32[2,60,128]{2,1,0:T(8,128)}), f32[2,60,128]{2,1,0:T(8,128)S(1)}, u32[]{:S(2)}, u32[]{:S(2)}) async-start(f32[2,60,128]{2,1,0:T(8,128)} %fold_step.1), calls=%async_computation.1 | async-start | bytes 131072 | tf_op jit(solution)/shard_map/all_to_all | solution.py:394
  66.6 0.1 pad_add_fusion.own_ref
  66.7 6.4 %rest_step.1 = f32[3,16384]{1,0:T(4,128)} custom-call(s32[3,16384]{1,0:T(4,128)S(1)} %copy-done, s32[1,512]{1,0:T(1,128)S(1)} %bitcast.16, f32[2,16384]{1,0:T(2,128)S(1)} %get-tuple-element.36.refs_2_.base_ref, f8e4m3fn[576,1536]{1,0:T(32,128)(4,1)S(1)} %get-tuple-element.32.refs_3_.table_ref, f32[2,8192]{1,0:T(2,128)S(1)} %first_step.1.flat_ref, ...), custom_call_target="tpu_custom_call" | custom-call | tf_op jit(solution)/shard_map/rest_step/pallas_call | solution.py:369
  73.1 6.4 %all-to-all-done.1.both_ref = f32[2,60,128]{2,1,0:T(8,128)S(1)} async-done(((f32[2,60,128]{2,1,0:T(8,128)}), f32[2,60,128]{2,1,0:T(8,128)S(1)}, u32[]{:S(2)}, u32[]{:S(2)}) %all-to-all-start.1) | async-done | bytes 61472 | tf_op jit(solution)/shard_map/all_to_all | solution.py:394
  79.4 1.2 %last_step.1 = (f32[2,2,1152]{2,1,0:T(2,128)}, f32[3,2,512]{2,1,0:T(2,128)}) custom-call(f32[2,60,128]{2,1,0:T(8,128)S(1)} %all-to-all-done.1.both_ref, f32[17,36,128]{2,1,0:T(8,128)S(1)} %collective-permute-done.2.carried_ref, f32[12,128]{1,0:T(8,128)S(1)} %collective-permute-done.3.fallen_ref, s32[3]{0:T(128)S(1)} %pad_add_fusion.own_ref), custom_call_target="tpu_custom_call" | custom-call | tf_op jit(solution)/shard_map/last_step/pallas_call | solution.py:369
  (1 shorter events, 0.0 us)
Async XLA Ops:
  2.2 9.1 %copy-start = (s32[3,16384]{1,0:T(4,128)S(1)}, s32[3,16384]{1,0:T(4,128)}, u32[]{:S(2)}) copy-start(s32[3,16384]{1,0:T(4,128)} %cells_ref.5) | copy-start | bytes 589828
  2.2 9.1 %copy-start.1 = (f32[3,16384]{1,0:T(4,128)S(1)}, f32[3,16384]{1,0:T(4,128)}, u32[]{:S(2)}) copy-start(f32[3,16384]{1,0:T(4,128)} %offsets_ref.3) | copy-start | bytes 589828
  2.2 9.1 %copy-start.2 = (f32[3,16384]{1,0:T(4,128)S(1)}, f32[3,16384]{1,0:T(4,128)}, u32[]{:S(2)}) copy-start(f32[3,16384]{1,0:T(4,128)} %displace_ref.3) | copy-start | bytes 589828
  2.3 9.0 %copy-start.3 = (s32[512]{0:T(512)S(1)}, s32[512]{0:T(512)}, u32[]{:S(2)}) copy-start(s32[512]{0:T(512)} %param.10) | copy-start | bytes 6148
  2.3 13.4 %collective-permute-start = (f32[2,288,128]{2,1,0:T(8,128)S(1)}, f32[2,288,128]{2,1,0:T(8,128)S(1)}, u32[]{:S(2)}, u32[]{:S(2)}) collective-permute-start(f32[2,288,128]{2,1,0:T(8,128)S(1)} %get-tuple-element.44), channel_id=1, source_target_pairs={{0,32},{1,33},{2,34},{3,35},{4,36},{5,37},{6,38},{7,39},{8,40},{9,... | collective-permute-start | bytes 884744 | tf_op jit(solution)/shard_map/ppermute | solution.py:404
  2.3 9.0 %copy-start.4 = (s32[1,2,16]{2,1,0:T(2,128)S(1)}, s32[1,2,16]{2,1,0:T(2,128)}, u32[]{:S(2)}) copy-start(s32[1,2,16]{2,1,0:T(2,128)} %chosen_ref.3) | copy-start | bytes 388
  2.3 9.0 %copy-start.5 = (s32[1,2]{1,0:T(1,128)S(1)}, s32[1,2]{1,0:T(1,128)}, u32[]{:S(2)}) copy-start(s32[1,2]{1,0:T(1,128)} %used_ref.3) | copy-start | bytes 28
  2.4 13.3 %collective-permute-start.1 = (f32[2,288,128]{2,1,0:T(8,128)S(1)}, f32[2,288,128]{2,1,0:T(8,128)S(1)}, u32[]{:S(2)}, u32[]{:S(2)}) collective-permute-start(f32[2,288,128]{2,1,0:T(8,128)S(1)} %get-tuple-element.43), channel_id=1, source_target_pairs={{0,484},{1,485},{2,486},{3,487},{4,480},{5,481},{6,482},{7,483},{8... | collective-permute-start | bytes 884744 | tf_op jit(solution)/shard_map/ppermute | solution.py:404
  31.5 8.0 %collective-permute-start.2 = (f32[17,36,128]{2,1,0:T(8,128)S(1)}, f32[17,36,128]{2,1,0:T(8,128)S(1)}, u32[]{:S(2)}, u32[]{:S(2)}) collective-permute-start(f32[17,36,128]{2,1,0:T(8,128)S(1)} %get-tuple-element.28), channel_id=1, source_target_pairs={{0,32},{1,33},{2,34},{3,35},{4,36},{5,37},{6,38},{7,39},{8,40},{9,... | collective-permute-start | bytes 940040 | tf_op jit(solution)/shard_map/ppermute | solution.py:404
  40.4 16.5 %all-to-all-start = ((f32[16,72,128]{2,1,0:T(8,128)}), f32[16,72,128]{2,1,0:T(8,128)S(1)}, u32[]{:S(2)}, u32[]{:S(2)}) async-start(f32[16,72,128]{2,1,0:T(8,128)} %merge_step.1), calls=%async_computation | async-start | bytes 1179648 | tf_op jit(solution)/shard_map/all_to_all | solution.py:394
  47.8 9.1 %collective-permute-start.3 = (f32[12,128]{1,0:T(8,128)S(1)}, f32[12,128]{1,0:T(8,128)S(1)}, u32[]{:S(2)}, u32[]{:S(2)}) collective-permute-start(f32[12,128]{1,0:T(8,128)S(1)} %get-tuple-element.34), channel_id=1, source_target_pairs={{0,484},{1,485},{2,486},{3,487},{4,480},{5,481},{6,482},{7,483},{8... | collective-permute-start | bytes 18440 | tf_op jit(solution)/shard_map/ppermute | solution.py:404
  57.6 21.9 %all-to-all-start.1 = ((f32[2,60,128]{2,1,0:T(8,128)}), f32[2,60,128]{2,1,0:T(8,128)S(1)}, u32[]{:S(2)}, u32[]{:S(2)}) async-start(f32[2,60,128]{2,1,0:T(8,128)} %fold_step.1), calls=%async_computation.1 | async-start | bytes 131072 | tf_op jit(solution)/shard_map/all_to_all | solution.py:394
